TPU v7x, 32 devices: a whole 2x2x4 slice. The times are simulated.
32 devices in a mesh: lat: 4 (over y, core), lon: 8 (over z, x).
Axes of the slice: x: 2, y: 2, z: 4, core: 2. Of those that a mesh axis runs over, the one named last changes fastest.
Arguments:
- background_expectation: float32 [3, 32, 1024], P(None, 'lat', 'lon'), may hold values from -6 to 6
- factor: float32 [32, 3, 32, 1024], P(None, None, 'lat', 'lon'), may hold values from -6 to 6
- average_thickness: float32 [32, 1024], P('lat', 'lon'), may hold values from 1 to 2
- obs_cells: int32 [8192], P(('lat', 'lon')), may hold values from 0 to 1023
- obs_count: int32 [32], P(('lat', 'lon')), may hold values from 64 to 256, as said below
- obs_values: float32 [8192], P(('lat', 'lon')), may hold values from -384 to 384
- obs_error: float32 [8192], P(('lat', 'lon')), may hold values from 20 to 200
Outputs:
- updated_expectation: float32 [3, 32, 1024], P(None, 'lat', 'lon')
- analysis_factor: float32 [32, 3, 32, 1024], P(None, None, 'lat', 'lon')
Inputs may be any that keep to these rules, and one draw needn't show every extreme that they name: `obs_cells`: each entry is a cell of the block of the device that holds the slot, row-major over its 8 x 128 cells. Device d uses its first obs_count[d] slots; some device uses all 256.
All inputs are finite; a program needn't handle non-finite values.
Results may differ from a plain program's by a relative error of at most 0.00027.
Values sent between devices are 32-bit elements; how exact they have to be, the bound alone decides.
A program may use at most 64 MiB of HBM per device.

v0:
```python
import jax
import jax.numpy as jnp
from jax import lax
from jax.sharding import PartitionSpec as P

STEPS = 4


TIME_STEP = 0.9
ROTATION = 0.25


def with_halo(block, sides, width, periodic):
    for axis, dim in sides:
        count = lax.axis_size(axis)
        forward = [(i, i + 1) for i in range(count - 1)]
        if periodic:
            forward.append((count - 1, 0))
        backward = [(target, source) for source, target in forward]
        low = lax.ppermute(
            lax.slice_in_dim(block, block.shape[dim] - width, None, axis=dim), axis, forward
        )
        high = lax.ppermute(lax.slice_in_dim(block, 0, width, axis=dim), axis, backward)
        block = jnp.concatenate([low, block, high], axis=dim)
    return block


def centred(field, axis):
    return 0.5 * (jnp.roll(field, -1, axis) - jnp.roll(field, 1, axis))


def advance(extended, row_mask):
    columns = (extended.shape[0] - 1) // 3
    state = extended[:-1].reshape(columns, 3, extended.shape[1], extended.shape[2])
    depth_plane = extended[-1]
    height, east_wind, north_wind = (state[:, 0], state[:, 1], state[:, 2])
    divergence = centred(east_wind, 2) + centred(north_wind, 1)
    height = (height - TIME_STEP * depth_plane * divergence) * row_mask
    new_east = (east_wind - TIME_STEP * centred(height, 2) + ROTATION * north_wind) * row_mask
    north_wind = (north_wind - TIME_STEP * centred(height, 1) - ROTATION * east_wind) * row_mask
    return jnp.stack([height, new_east, north_wind], 1)


def per_device(
    background_expectation, factor, average_thickness, obs_cells, obs_count, obs_values, obs_error
):
    band_rows = factor.shape[2]
    cycle_cols = factor.shape[3]
    columns = factor.shape[0] + 1
    joined_components = jnp.concatenate([background_expectation[None], factor], 0)
    depth_plane = average_thickness[None]
    for repeat in range(STEPS):
        extended = with_halo(
            jnp.concatenate(
                [joined_components.reshape(3 * columns, band_rows, cycle_cols), depth_plane], 0
            ),
            (("lat", 1),),
            2,
            False,
        )
        extended = with_halo(extended, (("lon", 2),), 2, True)
        global_row = lax.axis_index("lat") * band_rows - 2 + jnp.arange(band_rows + 2 * 2)
        inside = (global_row >= 0) & (global_row < band_rows * lax.axis_size("lat"))
        joined_components = advance(extended, inside.astype(jnp.float32)[:, None])[
            :, :, 2 : 2 + band_rows, 2 : 2 + cycle_cols
        ]
    surface_elevation = joined_components[:, 0].reshape(columns, band_rows * cycle_cols)
    picked = jnp.take(surface_elevation, obs_cells, axis=1)
    live = (jnp.arange(obs_cells.shape[0], dtype=jnp.int32) < obs_count[0]).astype(jnp.float32)
    weight = live / obs_error
    scaled = picked[1:] * weight
    innovation = (obs_values - picked[0]) * weight
    gram = jnp.dot(scaled, scaled.T, precision=lax.Precision.HIGHEST)
    drive = jnp.dot(scaled, innovation, precision=lax.Precision.HIGHEST)
    gram, drive = lax.psum((gram, drive), ("lat", "lon"))
    rank = columns - 1
    identity = jnp.eye(rank, dtype=jnp.float32)
    system = identity + gram
    lower = jnp.linalg.cholesky(system)
    inverse = lax.linalg.triangular_solve(
        lower, identity, left_side=True, lower=True, transpose_a=True
    )
    middle = lax.linalg.triangular_solve(lower, drive[:, None], left_side=True, lower=True)
    difference_coefficients = lax.linalg.triangular_solve(
        lower, middle, left_side=True, lower=True, transpose_a=True
    )[:, 0]
    sample_realisations = joined_components[1:].reshape(rank, -1)
    analysis_factor = jnp.dot(
        inverse.T, sample_realisations, precision=lax.Precision.HIGHEST
    ).reshape(factor.shape)
    updated_expectation = joined_components[0] + jnp.dot(
        difference_coefficients, sample_realisations, precision=lax.Precision.HIGHEST
    ).reshape(background_expectation.shape)
    return (updated_expectation, analysis_factor)


def solution(mesh):
    return jax.shard_map(
        per_device,
        mesh=mesh,
        in_specs=(
            P(None, "lat", "lon"),
            P(None, None, "lat", "lon"),
            P("lat", "lon"),
            P(("lat", "lon")),
            P(("lat", "lon")),
            P(("lat", "lon")),
            P(("lat", "lon")),
        ),
        out_specs=(P(None, "lat", "lon"), P(None, None, "lat", "lon")),
        check_vma=False,
    )
```

profile of v0, /device:TPU:0, one launch (start us, length us, event | category | flops | bytes accessed | tf_op | source)
XLA Modules:
  0.0 159.9 jit_solution(2461134982467058420)
XLA Ops:
  2.5 2.4 %collective-permute-start = (f32[100,2,128]{2,1,0:T(2,128)S(1)}, f32[100,2,128]{2,1,0:T(2,128)S(1)}, u32[]{:S(2)}, u32[]{:S(2)}) collective-permute-start(f32[100,2,128]{2,1,0:T(2,128)S(1)} %get-tuple-element.146), channel_id=1, source_target_pairs={{0,8},{8,16},{16,24},{1,9},{9,17},{17,25},{2,10},{10,18},{18,26},{... | collective-permute-start | bytes 307208 | tf_op jit(solution)/shard_map/ppermute | solution.py:20
  4.9 1.3 collective-permute-start.1
  6.2 4.0 %collective-permute-done.1 = f32[100,2,128]{2,1,0:T(2,128)S(1)} collective-permute-done((f32[100,2,128]{2,1,0:T(2,128)S(1)}, f32[100,2,128]{2,1,0:T(2,128)S(1)}, u32[]{:S(2)}, u32[]{:S(2)}) %collective-permute-start.1) | collective-permute-done | bytes 102432 | tf_op jit(solution)/shard_map/ppermute | solution.py:23
  12.0 4.5 %collective-permute-start.3 = (f32[100,12,2]{0,2,1:T(2,128)S(1)}, f32[100,12,2]{0,2,1:T(2,128)S(1)}, u32[]{:S(2)}, u32[]{:S(2)}) collective-permute-start(f32[100,12,2]{0,2,1:T(2,128)S(1)} %copy.207), channel_id=1, source_target_pairs={{1,0},{2,1},{3,2},{4,3},{5,4},{6,5},{7,6},{0,7},{9,8},{10,9},{11,1... | collective-permute-start | bytes 28808 | tf_op jit(solution)/shard_map/ppermute | solution.py:23
  16.5 6.4 %collective-permute-done.2 = f32[100,12,2]{0,2,1:T(2,128)S(1)} collective-permute-done((f32[100,12,2]{0,2,1:T(2,128)S(1)}, f32[100,12,2]{0,2,1:T(2,128)S(1)}, u32[]{:S(2)}, u32[]{:S(2)}) %collective-permute-start.2) | collective-permute-done | bytes 9632 | tf_op jit(solution)/shard_map/ppermute | solution.py:20
  23.8 1.1 fusion.3
  27.3 1.2 fusion.35
  31.4 3.8 %collective-permute-start.4 = (f32[100,2,128]{2,1,0:T(2,128)S(1)}, f32[100,2,128]{2,1,0:T(2,128)S(1)}, u32[]{:S(2)}, u32[]{:S(2)}) collective-permute-start(f32[100,2,128]{2,1,0:T(2,128)S(1)} %get-tuple-element.144), channel_id=1, source_target_pairs={{0,8},{8,16},{16,24},{1,9},{9,17},{17,25},{2,10},{10,18},{18,26},{... | collective-permute-start | bytes 307208 | tf_op jit(solution)/shard_map/ppermute | solution.py:20
  35.2 1.3 collective-permute-start.5
  36.5 2.7 %collective-permute-done.5 = f32[100,2,128]{2,1,0:T(2,128)S(1)} collective-permute-done((f32[100,2,128]{2,1,0:T(2,128)S(1)}, f32[100,2,128]{2,1,0:T(2,128)S(1)}, u32[]{:S(2)}, u32[]{:S(2)}) %collective-permute-start.5) | collective-permute-done | bytes 102432 | tf_op jit(solution)/shard_map/ppermute | solution.py:23
  40.3 4.9 %collective-permute-start.7 = (f32[100,12,2]{0,2,1:T(2,128)S(1)}, f32[100,12,2]{0,2,1:T(2,128)S(1)}, u32[]{:S(2)}, u32[]{:S(2)}) collective-permute-start(f32[100,12,2]{0,2,1:T(2,128)S(1)} %copy.230), channel_id=1, source_target_pairs={{1,0},{2,1},{3,2},{4,3},{5,4},{6,5},{7,6},{0,7},{9,8},{10,9},{11,1... | collective-permute-start | bytes 28808 | tf_op jit(solution)/shard_map/ppermute | solution.py:23
  45.2 1.2 collective-permute-done.6
  47.3 1.2 fusion.7
  52.3 4.0 %collective-permute-start.8 = (f32[100,2,128]{2,1,0:T(2,128)S(1)}, f32[100,2,128]{2,1,0:T(2,128)S(1)}, u32[]{:S(2)}, u32[]{:S(2)}) collective-permute-start(f32[100,2,128]{2,1,0:T(2,128)S(1)} %get-tuple-element.142), channel_id=1, source_target_pairs={{0,8},{8,16},{16,24},{1,9},{9,17},{17,25},{2,10},{10,18},{18,26},{... | collective-permute-start | bytes 307208 | tf_op jit(solution)/shard_map/ppermute | solution.py:20
  56.3 1.3 collective-permute-start.9
  57.6 2.5 %collective-permute-done.9 = f32[100,2,128]{2,1,0:T(2,128)S(1)} collective-permute-done((f32[100,2,128]{2,1,0:T(2,128)S(1)}, f32[100,2,128]{2,1,0:T(2,128)S(1)}, u32[]{:S(2)}, u32[]{:S(2)}) %collective-permute-start.9) | collective-permute-done | bytes 102432 | tf_op jit(solution)/shard_map/ppermute | solution.py:23
  61.2 4.8 %collective-permute-start.11 = (f32[100,12,2]{0,2,1:T(2,128)S(1)}, f32[100,12,2]{0,2,1:T(2,128)S(1)}, u32[]{:S(2)}, u32[]{:S(2)}) collective-permute-start(f32[100,12,2]{0,2,1:T(2,128)S(1)} %copy.250), channel_id=1, source_target_pairs={{1,0},{2,1},{3,2},{4,3},{5,4},{6,5},{7,6},{0,7},{9,8},{10,9},{11,1... | collective-permute-start | bytes 28808 | tf_op jit(solution)/shard_map/ppermute | solution.py:23
  66.0 6.4 %collective-permute-done.10 = f32[100,12,2]{0,2,1:T(2,128)S(1)} collective-permute-done((f32[100,12,2]{0,2,1:T(2,128)S(1)}, f32[100,12,2]{0,2,1:T(2,128)S(1)}, u32[]{:S(2)}, u32[]{:S(2)}) %collective-permute-start.10) | collective-permute-done | bytes 9632 | tf_op jit(solution)/shard_map/ppermute | solution.py:20
  73.3 1.2 fusion.11
  78.2 4.0 %collective-permute-start.12 = (f32[100,2,128]{2,1,0:T(2,128)S(1)}, f32[100,2,128]{2,1,0:T(2,128)S(1)}, u32[]{:S(2)}, u32[]{:S(2)}) collective-permute-start(f32[100,2,128]{2,1,0:T(2,128)S(1)} %get-tuple-element.140), channel_id=1, source_target_pairs={{0,8},{8,16},{16,24},{1,9},{9,17},{17,25},{2,10},{10,18},{18,26},{... | collective-permute-start | bytes 307208 | tf_op jit(solution)/shard_map/ppermute | solution.py:20
  82.2 1.3 collective-permute-start.13
  84.0 2.2 %collective-permute-done.13 = f32[100,2,128]{2,1,0:T(2,128)S(1)} collective-permute-done((f32[100,2,128]{2,1,0:T(2,128)S(1)}, f32[100,2,128]{2,1,0:T(2,128)S(1)}, u32[]{:S(2)}, u32[]{:S(2)}) %collective-permute-start.13) | collective-permute-done | bytes 102432 | tf_op jit(solution)/shard_map/ppermute | solution.py:23
  87.4 2.0 %collective-permute-start.14 = (f32[100,12,2]{0,2,1:T(2,128)S(1)}, f32[100,12,2]{0,2,1:T(2,128)S(1)}, u32[]{:S(2)}, u32[]{:S(2)}) collective-permute-start(f32[100,12,2]{0,2,1:T(2,128)S(1)} %copy.269), channel_id=1, source_target_pairs={{0,1},{1,2},{2,3},{3,4},{4,5},{5,6},{6,7},{7,0},{8,9},{9,10},{10,1... | collective-permute-start | bytes 28808 | tf_op jit(solution)/shard_map/ppermute | solution.py:20
  90.0 3.8 %collective-permute-done.14 = f32[100,12,2]{0,2,1:T(2,128)S(1)} collective-permute-done((f32[100,12,2]{0,2,1:T(2,128)S(1)}, f32[100,12,2]{0,2,1:T(2,128)S(1)}, u32[]{:S(2)}, u32[]{:S(2)}) %collective-permute-start.14) | collective-permute-done | bytes 9632 | tf_op jit(solution)/shard_map/ppermute | solution.py:20
  94.8 1.2 fusion.15
  101.9 1.9 %copy.289 = f32[33,1,8,128]{0,3,2,1:T(8,128)} copy(f32[33,1,8,128]{3,0,2,1:T(8,128)} %slice.565) | data formatting | bytes 270336 | tf_op jit(solution)/shard_map/slice | solution.py:67
  103.9 1.8 %gather_fusion = f32[256,33]{1,0:T(8,128)S(1)} fusion(f32[33,1024]{0,1:T(8,128)} %bitcast.264, s32[1024]{0:T(1024)S(1)} %pad_clamp_fusion), kind=kCustom, calls=%fused_computation | custom fusion | bytes 68608 | tf_op jit(solution)/shard_map/jit(_take)/gather | solution.py:68
  107.4 38.5 %all-reduce = (f32[32,32]{1,0:T(8,128)S(1)}, f32[32]{0:T(128)S(1)}) all-reduce(f32[32,32]{1,0:T(8,128)S(1)} %fusion.88, f32[32]{0:T(128)S(1)} %convolution_bitcast_fusion.3), channel_id=1, replica_groups=mesh['lat'=4,'lon'=8] {'lat','lon'}, use_global_device_ids=true, to_apply=%region_0.1 | all-reduce | flops 1056 | bytes 8448 | tf_op jit(solution)/shard_map/psum | solution.py:75
  146.0 2.9 %cholesky.18 = f32[32,32]{1,0:T(8,128)S(1)} custom-call(f32[32,32]{1,0:T(8,128)S(1)} %fusion.104), custom_call_target="Cholesky" | custom-call | tf_op jit(solution)/shard_map/jit(cholesky)/cholesky | solution.py:79
  150.2 2.4 %custom-call.10 = f32[1,32,32]{1,2,0:T(8,128)S(1)} custom-call(f32[1,32,32]{2,1,0:T(8,128)S(1)} %fusion.95), custom_call_target="InvertDiagBlocksLowerTriangular" | custom-call | tf_op jit(solution)/shard_map/triangular_solve | solution.py:84
  153.2 1.1 fusion.78
  154.6 1.5 fusion.81
  (151 shorter events, 37.1 us)
Async XLA Ops:
  2.5 3.7 %collective-permute-start = (f32[100,2,128]{2,1,0:T(2,128)S(1)}, f32[100,2,128]{2,1,0:T(2,128)S(1)}, u32[]{:S(2)}, u32[]{:S(2)}) collective-permute-start(f32[100,2,128]{2,1,0:T(2,128)S(1)} %get-tuple-element.146), channel_id=1, source_target_pairs={{0,8},{8,16},{16,24},{1,9},{9,17},{17,25},{2,10},{10,18},{18,26},{... | collective-permute-start | bytes 307208 | tf_op jit(solution)/shard_map/ppermute | solution.py:20
  4.9 5.3 %collective-permute-start.1 = (f32[100,2,128]{2,1,0:T(2,128)S(1)}, f32[100,2,128]{2,1,0:T(2,128)S(1)}, u32[]{:S(2)}, u32[]{:S(2)}) collective-permute-start(f32[100,2,128]{2,1,0:T(2,128)S(1)} %get-tuple-element.147), channel_id=1, source_target_pairs={{8,0},{16,8},{24,16},{9,1},{17,9},{25,17},{10,2},{18,10},{26,18},{... | collective-permute-start | bytes 307208 | tf_op jit(solution)/shard_map/ppermute | solution.py:23
  11.3 12.5 %copy-start.2 = (f32[8,128]{1,0:T(8,128)S(1)}, f32[8,128]{1,0:T(8,128)}, u32[]{:S(2)}) copy-start(f32[8,128]{1,0:T(8,128)} %param.9) | copy-start | bytes 12292
  12.0 11.4 %collective-permute-start.3 = (f32[100,12,2]{0,2,1:T(2,128)S(1)}, f32[100,12,2]{0,2,1:T(2,128)S(1)}, u32[]{:S(2)}, u32[]{:S(2)}) collective-permute-start(f32[100,12,2]{0,2,1:T(2,128)S(1)} %copy.207), channel_id=1, source_target_pairs={{1,0},{2,1},{3,2},{4,3},{5,4},{6,5},{7,6},{0,7},{9,8},{10,9},{11,1... | collective-permute-start | bytes 28808 | tf_op jit(solution)/shard_map/ppermute | solution.py:23
  16.5 6.4 %collective-permute-start.2 = (f32[100,12,2]{0,2,1:T(2,128)S(1)}, f32[100,12,2]{0,2,1:T(2,128)S(1)}, u32[]{:S(2)}, u32[]{:S(2)}) collective-permute-start(f32[100,12,2]{0,2,1:T(2,128)S(1)} %copy.206), channel_id=1, source_target_pairs={{0,1},{1,2},{2,3},{3,4},{4,5},{5,6},{6,7},{7,0},{8,9},{9,10},{10,1... | collective-permute-start | bytes 28808 | tf_op jit(solution)/shard_map/ppermute | solution.py:20
  31.4 5.1 %collective-permute-start.4 = (f32[100,2,128]{2,1,0:T(2,128)S(1)}, f32[100,2,128]{2,1,0:T(2,128)S(1)}, u32[]{:S(2)}, u32[]{:S(2)}) collective-permute-start(f32[100,2,128]{2,1,0:T(2,128)S(1)} %get-tuple-element.144), channel_id=1, source_target_pairs={{0,8},{8,16},{16,24},{1,9},{9,17},{17,25},{2,10},{10,18},{18,26},{... | collective-permute-start | bytes 307208 | tf_op jit(solution)/shard_map/ppermute | solution.py:20
  35.2 4.0 %collective-permute-start.5 = (f32[100,2,128]{2,1,0:T(2,128)S(1)}, f32[100,2,128]{2,1,0:T(2,128)S(1)}, u32[]{:S(2)}, u32[]{:S(2)}) collective-permute-start(f32[100,2,128]{2,1,0:T(2,128)S(1)} %get-tuple-element.145), channel_id=1, source_target_pairs={{8,0},{16,8},{24,16},{9,1},{17,9},{25,17},{10,2},{18,10},{26,18},{... | collective-permute-start | bytes 307208 | tf_op jit(solution)/shard_map/ppermute | solution.py:23
  40.0 6.4 %collective-permute-start.6 = (f32[100,12,2]{0,2,1:T(2,128)S(1)}, f32[100,12,2]{0,2,1:T(2,128)S(1)}, u32[]{:S(2)}, u32[]{:S(2)}) collective-permute-start(f32[100,12,2]{0,2,1:T(2,128)S(1)} %copy.229), channel_id=1, source_target_pairs={{0,1},{1,2},{2,3},{3,4},{4,5},{5,6},{6,7},{7,0},{8,9},{9,10},{10,1... | collective-permute-start | bytes 28808 | tf_op jit(solution)/shard_map/ppermute | solution.py:20
  40.3 6.5 %collective-permute-start.7 = (f32[100,12,2]{0,2,1:T(2,128)S(1)}, f32[100,12,2]{0,2,1:T(2,128)S(1)}, u32[]{:S(2)}, u32[]{:S(2)}) collective-permute-start(f32[100,12,2]{0,2,1:T(2,128)S(1)} %copy.230), channel_id=1, source_target_pairs={{1,0},{2,1},{3,2},{4,3},{5,4},{6,5},{7,6},{0,7},{9,8},{10,9},{11,1... | collective-permute-start | bytes 28808 | tf_op jit(solution)/shard_map/ppermute | solution.py:23
  52.3 5.3 %collective-permute-start.8 = (f32[100,2,128]{2,1,0:T(2,128)S(1)}, f32[100,2,128]{2,1,0:T(2,128)S(1)}, u32[]{:S(2)}, u32[]{:S(2)}) collective-permute-start(f32[100,2,128]{2,1,0:T(2,128)S(1)} %get-tuple-element.142), channel_id=1, source_target_pairs={{0,8},{8,16},{16,24},{1,9},{9,17},{17,25},{2,10},{10,18},{18,26},{... | collective-permute-start | bytes 307208 | tf_op jit(solution)/shard_map/ppermute | solution.py:20
  56.3 3.8 %collective-permute-start.9 = (f32[100,2,128]{2,1,0:T(2,128)S(1)}, f32[100,2,128]{2,1,0:T(2,128)S(1)}, u32[]{:S(2)}, u32[]{:S(2)}) collective-permute-start(f32[100,2,128]{2,1,0:T(2,128)S(1)} %get-tuple-element.143), channel_id=1, source_target_pairs={{8,0},{16,8},{24,16},{9,1},{17,9},{25,17},{10,2},{18,10},{26,18},{... | collective-permute-start | bytes 307208 | tf_op jit(solution)/shard_map/ppermute | solution.py:23
  60.5 5.4 %copy-start.3 = (s32[256]{0:T(256)S(1)}, s32[256]{0:T(256)}, u32[]{:S(2)}) copy-start(s32[256]{0:T(256)} %param.10) | copy-start | bytes 3076
  61.2 11.6 %collective-permute-start.11 = (f32[100,12,2]{0,2,1:T(2,128)S(1)}, f32[100,12,2]{0,2,1:T(2,128)S(1)}, u32[]{:S(2)}, u32[]{:S(2)}) collective-permute-start(f32[100,12,2]{0,2,1:T(2,128)S(1)} %copy.250), channel_id=1, source_target_pairs={{1,0},{2,1},{3,2},{4,3},{5,4},{6,5},{7,6},{0,7},{9,8},{10,9},{11,1... | collective-permute-start | bytes 28808 | tf_op jit(solution)/shard_map/ppermute | solution.py:23
  65.9 6.4 %collective-permute-start.10 = (f32[100,12,2]{0,2,1:T(2,128)S(1)}, f32[100,12,2]{0,2,1:T(2,128)S(1)}, u32[]{:S(2)}, u32[]{:S(2)}) collective-permute-start(f32[100,12,2]{0,2,1:T(2,128)S(1)} %copy.249), channel_id=1, source_target_pairs={{0,1},{1,2},{2,3},{3,4},{4,5},{5,6},{6,7},{7,0},{8,9},{9,10},{10,1... | collective-permute-start | bytes 28808 | tf_op jit(solution)/shard_map/ppermute | solution.py:20
  78.2 5.8 %collective-permute-start.12 = (f32[100,2,128]{2,1,0:T(2,128)S(1)}, f32[100,2,128]{2,1,0:T(2,128)S(1)}, u32[]{:S(2)}, u32[]{:S(2)}) collective-permute-start(f32[100,2,128]{2,1,0:T(2,128)S(1)} %get-tuple-element.140), channel_id=1, source_target_pairs={{0,8},{8,16},{16,24},{1,9},{9,17},{17,25},{2,10},{10,18},{18,26},{... | collective-permute-start | bytes 307208 | tf_op jit(solution)/shard_map/ppermute | solution.py:20
  82.2 4.0 %collective-permute-start.13 = (f32[100,2,128]{2,1,0:T(2,128)S(1)}, f32[100,2,128]{2,1,0:T(2,128)S(1)}, u32[]{:S(2)}, u32[]{:S(2)}) collective-permute-start(f32[100,2,128]{2,1,0:T(2,128)S(1)} %get-tuple-element.141), channel_id=1, source_target_pairs={{8,0},{16,8},{24,16},{9,1},{17,9},{25,17},{10,2},{18,10},{26,18},{... | collective-permute-start | bytes 307208 | tf_op jit(solution)/shard_map/ppermute | solution.py:23
  87.4 6.9 %collective-permute-start.15 = (f32[100,12,2]{0,2,1:T(2,128)S(1)}, f32[100,12,2]{0,2,1:T(2,128)S(1)}, u32[]{:S(2)}, u32[]{:S(2)}) collective-permute-start(f32[100,12,2]{0,2,1:T(2,128)S(1)} %copy.270), channel_id=1, source_target_pairs={{1,0},{2,1},{3,2},{4,3},{5,4},{6,5},{7,6},{0,7},{9,8},{10,9},{11,1... | collective-permute-start | bytes 28808 | tf_op jit(solution)/shard_map/ppermute | solution.py:23
  87.4 6.4 %collective-permute-start.14 = (f32[100,12,2]{0,2,1:T(2,128)S(1)}, f32[100,12,2]{0,2,1:T(2,128)S(1)}, u32[]{:S(2)}, u32[]{:S(2)}) collective-permute-start(f32[100,12,2]{0,2,1:T(2,128)S(1)} %copy.269), channel_id=1, source_target_pairs={{0,1},{1,2},{2,3},{3,4},{4,5},{5,6},{6,7},{7,0},{8,9},{9,10},{10,1... | collective-permute-start | bytes 28808 | tf_op jit(solution)/shard_map/ppermute | solution.py:20
  101.7 3.9 %copy-start.4 = (pred[256]{0:T(512)(128)(4,1)S(1)}, pred[256]{0:T(512)(128)(4,1)}, u32[]{:S(2)}) copy-start(pred[256]{0:T(512)(128)(4,1)} %compare_and_fusion) | copy-start | bytes 772
  152.7 1.6 %copy-start = (f32[33,1,12,1]{3,0,2,1:T(8,128)S(1)}, f32[33,1,12,1]{3,0,2,1:T(8,128)}, u32[]{:S(2)}) copy-start(f32[33,1,12,1]{3,0,2,1:T(8,128)} %get-tuple-element.60) | copy-start | bytes 4756
  152.7 1.6 %copy-start.1 = (f32[33,1,12,1]{3,0,2,1:T(8,128)S(1)}, f32[33,1,12,1]{3,0,2,1:T(8,128)}, u32[]{:S(2)}) copy-start(f32[33,1,12,1]{3,0,2,1:T(8,128)} %get-tuple-element.61) | copy-start | bytes 4756
where the time goes:
time: 162 us; the launch traced here: 160 us
  blocking collectives  38.5 us (24%)
  starting transfers between devices  35.5 us (22%)
  waiting for transfers between devices  29.1 us (18%)
  other arithmetic  28.8 us (18%)
  local copies, waits for them, and re-layouts  23.6 us (15%)
  matrix products  2.15 us (1%)
  between operations  2.14 us (1%)
    psum x1, blocking collectives, per_device(): gram, drive = lax.psum((gram, drive), ('lat', 'lon'))  38.5 us
    ppermute x8, starting transfers between devices, with_halo(): lax.ppermute(lax.slice_in_dim(block, 0, width, axis=dim), axis, backward)  19.4 us
    ppermute x8, waiting for transfers between devices, with_halo(): lax.ppermute(lax.slice_in_dim(block, block.shape[dim] - width, None, axis...  17.7 us
    ppermute x8, starting transfers between devices, with_halo(): lax.ppermute(lax.slice_in_dim(block, block.shape[dim] - width, None, axis...  16.2 us
    ppermute x8, waiting for transfers between devices, with_halo(): lax.ppermute(lax.slice_in_dim(block, 0, width, axis=dim), axis, backward)  11.4 us
    concatenate x8, other arithmetic, with_halo(): block = jnp.concatenate([low, block, high], axis=dim)  5.93 us
    concatenate x32, local copies, waits for them, and re-layouts, centred(): return 0.5 * (jnp.roll(field, -1, axis) - jnp.roll(field, 1, axis))  5.54 us
    mul x4, other arithmetic, advance(): (east_wind - TIME_STEP * centred(height, 2) + ROTATION * north_wind) * ro...  4.29 us
  transfers between devices with their start and end apart: 16, of which 8 were waited for; matrix products, arithmetic and copies ran while one was open for 2% of the time, Pallas kernels for 0%

commit v1 on v0

v1 whole, which is shorter than its diff:
```python
import functools

import jax
import jax.numpy as jnp
from jax import lax
from jax.experimental import pallas as pl
from jax.experimental.pallas import tpu as pltpu
from jax.sharding import PartitionSpec as P

STEPS = 4
TIME_STEP = 0.9
ROTATION = 0.25
MESH = pl.DeviceIdType.MESH
T = 8
NT = (((1,), (1,)), ((), ()))
HIGHEST = lax.Precision.HIGHEST


def roll(x, shift, axis=1):
    shift = shift % x.shape[axis]
    return x if shift == 0 else pltpu.roll(x, shift, axis)


def evolve(h, e, n, coef, up_gain, down_gain, band):
    half = 0.5 * TIME_STEP
    for step in range(STEPS):
        w = 2 * (STEPS - step)
        last = coef.shape[0] - T * (band - w + 1)
        mid = e[T:-T]
        div = (roll(mid, -1) - roll(mid, 1)) + (n[2 * T :] - n[: -2 * T])
        hn = h[T:-T] - coef[T * (band - w + 1) : last] * div
        inner = hn[T:-T]
        shape = (T * (w - 2), h.shape[1])
        parts = [jnp.full((T * band, h.shape[1]), half, jnp.float32)]
        if w > 2:
            parts = [jnp.full(shape, up_gain)] + parts + [jnp.full(shape, down_gain)]
        gain = jnp.concatenate(parts, 0) if w > 2 else parts[0]
        e0, n0 = e[2 * T : -2 * T], n[2 * T : -2 * T]
        e = e0 - half * (roll(inner, -1) - roll(inner, 1)) + ROTATION * n0
        n = n0 - gain * (hn[2 * T :] - hn[: -2 * T]) - ROTATION * e0
        h = inner
    return h, e, n


def kernel(
    n_lat, n_lon, rank,
    mean_ref, fac_ref, depth_ref, cells_ref, count_ref, vals_ref, err_ref,
    upd_ref, out_ref,
    up_buf, dn_buf, aux, aux_up, aux_dn, edge_right, edge_left, from_left, from_right,
    fc, gt, p1, p2, ar1, ar2,
    s_main, r_main, s_aux, r_aux, s_el, r_el, s_er, r_er, s1, r1, s2, r2,
):
    lat, lon = lax.axis_index("lat"), lax.axis_index("lon")
    band, lanes = depth_ref.shape
    groups = rank // T
    slot = lanes // groups
    half_slot = slot // 2
    edge = 2 * STEPS
    per = 3 * band
    chunk = T * per
    lane8 = lax.broadcasted_iota(jnp.int32, (T, lanes), 1)
    sub8 = lax.broadcasted_iota(jnp.int32, (T, lanes), 0)

    def at(dlat, dlon):
        return (lax.rem(lat + dlat + n_lat, n_lat), lax.rem(lon + dlon + n_lon, n_lon))

    diagonals = [(a, b) for a in (-1, 1) for b in (-1, 1)]
    peers = [(a, 0) for a in range(1, n_lat)] + [(0, b) for b in range(1, n_lon)] + diagonals
    barrier = pltpu.get_barrier_semaphore()
    for a, b in peers:
        pl.semaphore_signal(barrier, inc=1, device_id=at(a, b), device_id_type=MESH)

    has_up, has_dn = lat > 0, lat < n_lat - 1
    aux[0 : 3 * band, :] = mean_ref[...]
    aux[3 * band :, :] = depth_ref[...]

    @pl.when(jnp.logical_not(has_up))
    def _():
        up_buf[...] = jnp.zeros_like(up_buf)
        aux_up[...] = jnp.zeros_like(aux_up)
        from_left[0] = jnp.zeros_like(from_left[0])
        from_right[0] = jnp.zeros_like(from_right[0])

    @pl.when(jnp.logical_not(has_dn))
    def _():
        dn_buf[...] = jnp.zeros_like(dn_buf)
        aux_dn[...] = jnp.zeros_like(aux_dn)
        from_left[2] = jnp.zeros_like(from_left[2])
        from_right[2] = jnp.zeros_like(from_right[2])

    def remote(src, dst, ssem, rsem, where):
        return pltpu.make_async_remote_copy(
            src_ref=src, dst_ref=dst, send_sem=ssem, recv_sem=rsem, device_id=where, device_id_type=MESH
        )

    def main_copy(side, g):
        rows = pl.ds(g * chunk, chunk)
        dst = (up_buf, dn_buf)[side]
        return remote(fac_ref.at[rows], dst.at[rows], s_main.at[side, g], r_main.at[side, g], at(1 - 2 * side, 0))

    def aux_copy(side):
        dst = (aux_up, aux_dn)[side]
        return remote(aux, dst, s_aux.at[side], r_aux.at[side], at(1 - 2 * side, 0))

    def edge_copy(to_right, block):
        dlat = 1 - block
        if to_right:
            return remote(edge_right, from_left.at[block], s_er.at[block], r_er.at[block], at(dlat, 1))
        return remote(edge_left, from_right.at[block], s_el.at[block], r_el.at[block], at(dlat, -1))

    sends = (has_dn, has_up)
    receives = (has_up, has_dn)

    pl.semaphore_wait(barrier, len(peers))
    for side in range(2):
        @pl.when(sends[side])
        def _(side=side):
            aux_copy(side).start()
            for g in range(groups):
                main_copy(side, g).start()

    def load(ref, f, g):
        return jnp.concatenate([ref[pl.ds(g * chunk + f * band + r, T, stride=per), :] for r in range(band)], 0)

    stack_lane = lax.broadcasted_iota(jnp.int32, (T * band, lanes), 1)
    stack_sub = lax.broadcasted_iota(jnp.int32, (T * band, lanes), 0)

    def seam_tiles(ref, f):
        tiles = roll(load(ref, f, groups - 1), slot * (groups - 1) + half_slot)
        for g in range(groups - 1):
            tiles = jnp.where(
                (stack_lane >= slot * g) & (stack_lane < slot * (g + 1)),
                roll(load(ref, f, g), slot * g + half_slot),
                tiles,
            )
        return tiles

    fold = slot // edge
    own_seams = []
    tiles_per = band // fold
    in_slot = lax.rem(lane8, slot)
    for f in range(3):
        seams = seam_tiles(fac_ref, f)
        own_seams.append(seams)
        for t in range(tiles_per):
            right = left = None
            for q in range(fold):
                tile = seams[T * (t * fold + q) : T * (t * fold + q + 1)]
                to_right = roll(tile, edge * q - (half_slot - edge))
                to_left = roll(tile, edge * q - half_slot)
                keep = (in_slot >= edge * q) & (in_slot < edge * (q + 1))
                right = to_right if q == 0 else jnp.where(keep, to_right, right)
                left = to_left if q == 0 else jnp.where(keep, to_left, left)
            row = T * (f * tiles_per + t)
            edge_right[row : row + T, :] = right
            edge_left[row : row + T, :] = left
    aux_edge = None
    for f in range(4):
        tile = roll(aux[f * band : (f + 1) * band, :], 2 * edge * f + edge)
        aux_edge = tile if f == 0 else jnp.where(lane8 >= 2 * edge * f, tile, aux_edge)
    edge_rows = T * 3 * tiles_per
    edge_right[edge_rows:, :] = aux_edge
    edge_left[edge_rows:, :] = aux_edge

    for block in (1, 0, 2):
        def go(block=block):
            edge_copy(True, block).start()
            edge_copy(False, block).start()
        if block == 1:
            go()
        else:
            pl.when(sends[0] if block == 0 else sends[1])(go)

    cells = cells_ref[...]
    slots = cells.shape[1]
    live = lax.broadcasted_iota(jnp.int32, (1, slots), 1) < count_ref[...]
    weight = jnp.where(live, 1.0, 0.0) / err_ref[...]
    square = weight * weight
    obs_row = jnp.zeros_like(cells)
    for r in range(1, band):
        obs_row = obs_row + jnp.where(cells >= r * lanes, 1, 0)
    obs_col = cells - lanes * obs_row
    row_hot = lax.broadcasted_iota(jnp.int32, (band, slots), 0) == obs_row
    left_side = jnp.concatenate(
        [jnp.where(row_hot, square, 0.0), jnp.where(row_hot, square * vals_ref[...], 0.0)], 0
    )
    col_hot = jnp.where(lax.broadcasted_iota(jnp.int32, (lanes, slots), 0) == obs_col, 1.0, 0.0)
    cell_sums = lax.dot_general(left_side, col_hot, NT, precision=HIGHEST, preferred_element_type=jnp.float32)
    cell_weight, cell_value = cell_sums[:band], cell_sums[band:]

    half = 0.5 * TIME_STEP
    up_gain = jnp.where(has_up, half, 0.0).astype(jnp.float32)
    down_gain = jnp.where(has_dn, half, 0.0).astype(jnp.float32)

    def spread(tile):
        return jnp.concatenate([jnp.broadcast_to(tile[r : r + 1], (T, lanes)) for r in range(band)], 0)

    for side in range(2):
        @pl.when(receives[side])
        def _(side=side):
            aux_copy(side).wait_recv()
    aux_blocks = (aux_up, aux, aux_dn)
    coef = jnp.concatenate([half * spread(b[3 * band :, :]) for b in aux_blocks], 0)

    blocks = (up_buf, fac_ref, dn_buf)
    for g in range(groups):
        for side in range(2):
            @pl.when(receives[side])
            def _(side=side, g=g):
                main_copy(side, g).wait_recv()
        state = [jnp.concatenate([load(b, f, g) for b in blocks], 0) for f in range(3)]
        state = evolve(*state, coef, up_gain, down_gain, band)
        for f in range(3):
            for r in range(band):
                fc[f * band + r, T * g : T * (g + 1), :] = state[f][T * r : T * (r + 1)]

    edge_copy(True, 1).wait_recv()
    edge_copy(False, 1).wait_recv()
    for side in range(2):
        @pl.when(receives[side])
        def _(side=side):
            edge_copy(True, 2 * side).wait_recv()
            edge_copy(False, 2 * side).wait_recv()

    def aux_pair(b, f):
        own = aux_blocks[b][f * band : (f + 1) * band, :]
        left = from_left[b, edge_rows:, :]
        right = from_right[b, edge_rows:, :]
        strips = jnp.where(lane8 < half_slot, roll(left, half_slot - edge - 2 * edge * f), roll(own, half_slot))
        strips = jnp.where(
            lane8 < slot,
            strips,
            jnp.where(lane8 < slot + half_slot, roll(own, slot + half_slot), roll(right, slot + half_slot - edge - 2 * edge * f)),
        )
        return own, strips

    def mean_group(b, f):
        own, strips = aux_pair(b, f)
        return jnp.concatenate([jnp.where(sub8 == 0, own[r : r + 1], strips[r : r + 1]) for r in range(band)], 0)

    mean_state = [jnp.concatenate([mean_group(b, f) for b in range(3)], 0) for f in range(4)]
    mean_state = evolve(*mean_state[:3], half * mean_state[3], up_gain, down_gain, band)
    mean = []
    for f in range(3):
        strips = roll(mean_state[f], -1, 0)
        low = roll(strips, -half_slot)
        high = roll(strips, lanes - half_slot - slot)
        mean.append(jnp.where(stack_lane < edge, low, jnp.where(stack_lane >= lanes - edge, high, mean_state[f])))

    def repeat_slots(tile):
        tile = jnp.where(lane8 < slot, tile, 0.0)
        total = tile
        for g in range(1, groups):
            total = total + roll(tile, slot * g)
        return total

    strips_of = [aux_pair(b, 3)[1] for b in range(3)]
    coef_left = jnp.concatenate([half * spread(repeat_slots(s)) for s in strips_of], 0)
    coef_right = jnp.concatenate([half * spread(repeat_slots(roll(s, -slot))) for s in strips_of], 0)

    def unpack(ref, b, f, first):
        out = []
        for r in range(band):
            row = T * (f * tiles_per + r // fold)
            out.append(roll(ref[b, row : row + T, :], first - edge * (r % fold)))
        return jnp.concatenate(out, 0)

    low_half = lax.rem(stack_lane, slot) < half_slot
    left_state, right_state = [], []
    for f in range(3):
        lefts, rights = [], []
        for b in range(3):
            seams = own_seams[f] if b == 1 else seam_tiles(blocks[b], f)
            lefts.append(jnp.where(low_half, unpack(from_left, b, f, half_slot - edge), seams))
            rights.append(jnp.where(low_half, seams, unpack(from_right, b, f, half_slot)))
        left_state.append(jnp.concatenate(lefts, 0))
        right_state.append(jnp.concatenate(rights, 0))
    left_state = evolve(*left_state, coef_left, up_gain, down_gain, band)
    right_state = evolve(*right_state, coef_right, up_gain, down_gain, band)
    at_edge = (lane8 < edge) | (lane8 >= lanes - edge)
    for f in range(3):
        seams = jnp.where(low_half, right_state[f], left_state[f])
        for g in range(groups):
            back = roll(seams, -(slot * g + half_slot))
            for r in range(band):
                spot = (f * band + r, slice(T * g, T * (g + 1)), slice(None))
                fc[spot] = jnp.where(at_edge, back[T * r : T * (r + 1)], fc[spot])

    lhs, rhs = [], []
    for r in range(band):
        height = fc[r]
        w = cell_weight[r : r + 1]
        drive = cell_value[r : r + 1] - w * mean[0][T * r : T * r + 1]
        lhs.append(height)
        rhs.append(jnp.concatenate([height * w, jnp.where(sub8 == 0, drive, 0.0)], 0))
    gram = lax.dot_general(
        jnp.concatenate(lhs, 1), jnp.concatenate(rhs, 1), NT, precision=HIGHEST, preferred_element_type=jnp.float32
    )
    gt[...] = jnp.zeros_like(gt)
    gt[:, 0 : rank + T] = gram
    hr = rank // 2
    wide = lax.broadcasted_iota(jnp.int32, (hr, lanes), 1)
    mine = jnp.where(wide < lanes // 2, gt[0:hr, :], roll(gt[hr:, :], lanes // 2))

    p1[...] = mine
    def lat_copy(o):
        return remote(p1, ar1.at[o - 1], s1.at[o - 1], r1.at[o - 1], at(o, 0))
    def lon_copy(o):
        return remote(p2, ar2.at[o - 1], s2.at[o - 1], r2.at[o - 1], at(0, o))
    for o in range(1, n_lat):
        lat_copy(o).start()
    for o in range(1, n_lat):
        lat_copy(o).wait_recv()
        mine = mine + ar1[o - 1]
    p2[...] = mine
    for o in range(1, n_lon):
        lon_copy(o).start()
    for o in range(1, n_lon):
        lon_copy(o).wait_recv()
        mine = mine + ar2[o - 1]

    both = jnp.concatenate([mine, roll(mine, lanes // 2)], 0)
    ri = lax.broadcasted_iota(jnp.int32, (rank, lanes), 0)
    li = lax.broadcasted_iota(jnp.int32, (rank, lanes), 1)
    eyes = jnp.where((li == ri) | (li == ri + lanes // 2), 1.0, 0.0)
    x = jnp.where(li < lanes // 2, both, 0.0) + eyes
    tiles = [x[T * i : T * (i + 1)] for i in range(groups)]
    for j in range(rank):
        tj, sj = j // T, j % T
        row = tiles[tj][sj : sj + 1]
        inv = 1.0 / row[:, j : j + 1]
        scaled_row = row * inv
        for i in range(tj, groups):
            if i == tj and sj == T - 1:
                continue
            col = tiles[i][:, j : j + 1]
            if i == tj:
                col = jnp.where(sub8[:, :1] > sj, col, 0.0)
            tiles[i] = tiles[i] - col * scaled_row
    x = jnp.concatenate(tiles, 0)
    pivot = jnp.sum(jnp.where(li == ri, x, 0.0), 1, keepdims=True)
    x = x / jnp.sqrt(pivot)
    inverse = jnp.where(li < rank, roll(x, -(lanes // 2)), 0.0)
    z = x[:, rank : rank + 1]
    shift = jnp.sum(inverse * z, 0, keepdims=True)
    coefs = jnp.concatenate([inverse, jnp.where(sub8 == 0, shift, 0.0)], 0)[:, :rank]

    for f in range(3):
        slab = jnp.concatenate([fc[f * band + r] for r in range(band)], 1)
        res = jnp.dot(coefs, slab, precision=HIGHEST, preferred_element_type=jnp.float32)
        for r in range(band):
            part = res[:, lanes * r : lanes * (r + 1)]
            i = f * band + r
            for g in range(groups):
                out_ref[pl.ds(g * chunk + i, T, stride=per), :] = part[T * g : T * (g + 1)]
            upd_ref[i : i + 1, :] = mean[f][T * r : T * r + 1] + part[rank : rank + 1]

    for side in range(2):
        @pl.when(sends[side])
        def _(side=side):
            aux_copy(side).wait_send()
            for g in range(groups):
                main_copy(side, g).wait_send()
            edge_copy(True, 2 * side).wait_send()
            edge_copy(False, 2 * side).wait_send()
    edge_copy(True, 1).wait_send()
    edge_copy(False, 1).wait_send()
    for o in range(1, n_lat):
        lat_copy(o).wait_send()
    for o in range(1, n_lon):
        lon_copy(o).wait_send()


def per_device(n_lat, n_lon, background, factor, depth, cells, count, values, error):
    rank, fields, band, lanes = factor.shape
    groups = rank // T
    rows = rank * fields * band
    slots = cells.shape[0]
    assert band == T and 2 * STEPS <= band and rank % T == 0 and fields == 3
    edge_rows = T * (fields * band * groups * 2 * STEPS // lanes + 1)
    vmem = pl.BlockSpec(memory_space=pltpu.VMEM)
    f32 = functools.partial(pltpu.VMEM, dtype=jnp.float32)
    dma = pltpu.SemaphoreType.DMA
    updated, analysis = pl.pallas_call(
        functools.partial(kernel, n_lat, n_lon, rank),
        out_shape=(
            jax.ShapeDtypeStruct((fields * band, lanes), jnp.float32),
            jax.ShapeDtypeStruct((rows, lanes), jnp.float32),
        ),
        in_specs=[vmem] * 7,
        out_specs=(vmem, vmem),
        scratch_shapes=[
            f32((rows, lanes)), f32((rows, lanes)),
            f32((4 * band, lanes)), f32((4 * band, lanes)), f32((4 * band, lanes)),
            f32((edge_rows, lanes)), f32((edge_rows, lanes)),
            f32((3, edge_rows, lanes)), f32((3, edge_rows, lanes)),
            f32((fields * band, rank, lanes)), f32((rank, lanes)),
            f32((rank // 2, lanes)), f32((rank // 2, lanes)),
            f32((n_lat - 1, rank // 2, lanes)), f32((n_lon - 1, rank // 2, lanes)),
            dma((2, groups)), dma((2, groups)), dma((2,)), dma((2,)),
            dma((3,)), dma((3,)), dma((3,)), dma((3,)),
            dma((n_lat - 1,)), dma((n_lat - 1,)), dma((n_lon - 1,)), dma((n_lon - 1,)),
        ],
        compiler_params=pltpu.CompilerParams(
            collective_id=0, has_side_effects=True, vmem_limit_bytes=32 * 1024 * 1024
        ),
    )(
        background.reshape(fields * band, lanes), factor.reshape(rows, lanes), depth,
        cells.reshape(1, slots), count.reshape(1, 1), values.reshape(1, slots), error.reshape(1, slots),
    )
    return updated.reshape(background.shape), analysis.reshape(factor.shape)


def solution(mesh):
    return jax.shard_map(
        functools.partial(per_device, mesh.shape["lat"], mesh.shape["lon"]),
        mesh=mesh,
        in_specs=(
            P(None, "lat", "lon"),
            P(None, None, "lat", "lon"),
            P("lat", "lon"),
            P(("lat", "lon")),
            P(("lat", "lon")),
            P(("lat", "lon")),
            P(("lat", "lon")),
        ),
        out_specs=(P(None, "lat", "lon"), P(None, None, "lat", "lon")),
        check_vma=False,
    )
```

time: 162 us -> 32.4 us (0.20); the launches traced: 160 us -> 32.1 us
  blocking collectives: 38.5 us -> 0 us
  starting transfers between devices: 35.5 us -> 0 us
  waiting for transfers between devices: 29.1 us -> 0 us
  other arithmetic: 28.8 us -> 0 us
  Pallas kernels: 0 us -> 25.7 us
  local copies, waits for them, and re-layouts: 23.6 us -> 5.06 us
  matrix products: 2.15 us -> 0 us
    psum x1 -> x0, blocking collectives: 38.5 us -> none  [per_device(): gram, drive = lax.psum((gram, drive), ('lat', 'lon'))]
    ppermute x16 -> x0, starting transfers between devices: 35.5 us -> none  [the longest x8 19.4 us: with_halo(): lax.ppermute(lax.slice_in_dim(block, 0, width, axis=dim), axis, backward)]
    ppermute x16 -> x0, waiting for transfers between devices: 29.1 us -> none  [the longest x8 17.7 us: with_halo(): lax.ppermute(lax.slice_in_dim(block, block.shape[dim] - width, None, axis...]
    pallas_call x0 -> x1, Pallas kernels: none -> 25.7 us  [per_device(): pl.pallas_call(functools.partial(kernel, n_lat, n_lon, rank), out_shape=(...]
    mul x21 -> x0, other arithmetic: 11.2 us -> none  [the longest x4 4.29 us: advance(): (east_wind - TIME_STEP * centred(height, 2) + ROTATION * north_wind) * ro...]
    another operation x9 -> x0, other arithmetic: 8.86 us -> none  [the longest x3 3.59 us: per_device(): lower = jnp.linalg.cholesky(system)]
    concatenate x13 -> x0, other arithmetic: 7.98 us -> none  [the longest x8 5.93 us: with_halo(): block = jnp.concatenate([low, block, high], axis=dim)]
    slice x27 -> x0, local copies, waits for them, and re-layouts: 7.94 us -> none  [the longest x2 2.72 us: per_device(): joined_components[:, 0].reshape(columns, band_rows * cycle_cols)]
  transfers between devices with their start and end apart: 16 -> 0, of which waited for: 8 -> 0; matrix products, arithmetic and copies ran while one was open for 2% -> 0% of each run, Pallas kernels for 0% -> 0%
where the time goes in v1:
time: 32.4 us; the launch traced here: 32.1 us
  Pallas kernels  25.7 us (79%)
  local copies, waits for them, and re-layouts  5.06 us (16%)
  between operations  1.32 us (4%)
    pallas_call x1, Pallas kernels, per_device(): pl.pallas_call(functools.partial(kernel, n_lat, n_lon, rank), out_shape=(...  25.7 us
    unnamed x14, local copies, waits for them, and re-layouts  5.06 us

profile of v1, /device:TPU:0, one launch (start us, length us, event | category | flops | bytes accessed | tf_op | source)
XLA Modules:
  0.0 32.1 jit_solution(4434472907887688414)
XLA Ops:
  0.6 0.0 copy-start.1
  1.3 0.0 copy-start.3
  1.3 0.0 copy-done.1
  1.3 0.6 %copy-done.3 = s32[256]{0:T(256)S(1)} copy-done((s32[256]{0:T(256)S(1)}, s32[256]{0:T(256)}, u32[]{:S(2)}) %copy-start.3) | copy-done | bytes 1048
  2.0 0.0 copy-start
  2.0 1.0 %copy-done = f32[32,3,8,128]{3,2,1,0:T(8,128)S(1)} copy-done((f32[32,3,8,128]{3,2,1,0:T(8,128)S(1)}, f32[32,3,8,128]{3,2,1,0:T(8,128)}, u32[]{:S(2)}) %copy-start) | copy-done | bytes 393240
  3.0 0.0 copy-start.2
  3.0 0.7 %copy-done.2 = f32[8,128]{1,0:T(8,128)S(1)} copy-done((f32[8,128]{1,0:T(8,128)S(1)}, f32[8,128]{1,0:T(8,128)}, u32[]{:S(2)}) %copy-start.2) | copy-done | bytes 4120
  3.7 0.0 copy-start.4
  3.7 0.7 %copy-done.4 = f32[256]{0:T(256)S(1)} copy-done((f32[256]{0:T(256)S(1)}, f32[256]{0:T(256)}, u32[]{:S(2)}) %copy-start.4) | copy-done | bytes 1048
  4.3 0.0 copy-start.5
  4.3 0.7 %copy-done.5 = f32[256]{0:T(256)S(1)} copy-done((f32[256]{0:T(256)S(1)}, f32[256]{0:T(256)}, u32[]{:S(2)}) %copy-start.5) | copy-done | bytes 1048
  5.0 25.7 %shard_map.86 = (f32[24,128]{1,0:T(8,128)S(1)}, f32[768,128]{1,0:T(8,128)S(1)}) custom-call(f32[24,128]{1,0:T(8,128)S(1)} %bitcast.11, f32[768,128]{1,0:T(8,128)S(1)} %bitcast.9, f32[8,128]{1,0:T(8,128)S(1)} %copy-done.2, s32[1,256]{1,0:T(1,128)S(1)} %bitcast.13, s32[1,1]{1,0:T(1,128)} %bitcast.8.count_ref, f32[1,256]{1,0:T(1,128)S(1)} %bitcast.14, ...), custom_call_target="tpu_custom_call" | custom-call | tf_op jit(solution)/shard_map/pallas_call | solution.py:384
  30.7 0.6 %copy.12 = f32[3,8,128]{2,1,0:T(8,128)} copy(f32[3,8,128]{2,1,0:T(8,128)S(1)} %bitcast.12) | data formatting | bytes 24576
  31.3 0.7 %copy.13 = f32[32,3,8,128]{3,2,1,0:T(8,128)} copy(f32[32,3,8,128]{3,2,1,0:T(8,128)S(1)} %bitcast.10) | data formatting | bytes 786432
Async XLA Ops:
  0.6 0.7 %copy-start.1 = (f32[3,8,128]{2,1,0:T(8,128)S(1)}, f32[3,8,128]{2,1,0:T(8,128)}, u32[]{:S(2)}) copy-start(f32[3,8,128]{2,1,0:T(8,128)} %param.7) | copy-start | bytes 36868
  1.3 0.7 %copy-start.3 = (s32[256]{0:T(256)S(1)}, s32[256]{0:T(256)}, u32[]{:S(2)}) copy-start(s32[256]{0:T(256)} %param.10) | copy-start | bytes 3076
  2.0 1.0 %copy-start = (f32[32,3,8,128]{3,2,1,0:T(8,128)S(1)}, f32[32,3,8,128]{3,2,1,0:T(8,128)}, u32[]{:S(2)}) copy-start(f32[32,3,8,128]{3,2,1,0:T(8,128)} %param.8) | copy-start | bytes 1179652
  3.0 0.7 %copy-start.2 = (f32[8,128]{1,0:T(8,128)S(1)}, f32[8,128]{1,0:T(8,128)}, u32[]{:S(2)}) copy-start(f32[8,128]{1,0:T(8,128)} %depth_ref.1) | copy-start | bytes 12292
  3.7 0.7 %copy-start.4 = (f32[256]{0:T(256)S(1)}, f32[256]{0:T(256)}, u32[]{:S(2)}) copy-start(f32[256]{0:T(256)} %param.12) | copy-start | bytes 3076
  4.3 0.7 %copy-start.5 = (f32[256]{0:T(256)S(1)}, f32[256]{0:T(256)}, u32[]{:S(2)}) copy-start(f32[256]{0:T(256)} %param.13) | copy-start | bytes 3076

commit v2 on v1

--- a/solution.py
+++ b/solution.py
@@ -13,12 +13,20 @@
 MESH = pl.DeviceIdType.MESH
 T = 8
 NT = (((1,), (1,)), ((), ()))
-HIGHEST = lax.Precision.HIGHEST
 
 
 def roll(x, shift, axis=1):
     shift = shift % x.shape[axis]
     return x if shift == 0 else pltpu.roll(x, shift, axis)
+
+
+def split(x, terms):
+    parts = []
+    for _ in range(terms):
+        part = x.astype(jnp.bfloat16)
+        parts.append(part)
+        x = x - part.astype(jnp.float32)
+    return parts
 
 
 def evolve(h, e, n, coef, up_gain, down_gain, band):
@@ -44,14 +52,15 @@
 
 def kernel(
     n_lat, n_lon, rank,
-    mean_ref, fac_ref, depth_ref, cells_ref, count_ref, vals_ref, err_ref,
-    upd_ref, out_ref,
+    mean_hbm, fac_hbm, depth_hbm, cells_hbm, count_hbm, vals_hbm, err_hbm,
+    fc, mean_out, gram_out,
+    fac_ref, cells_ref, count_ref, vals_ref, err_ref, s_in,
     up_buf, dn_buf, aux, aux_up, aux_dn, edge_right, edge_left, from_left, from_right,
-    fc, gt, p1, p2, ar1, ar2,
+    p1, p2, ar1, ar2,
     s_main, r_main, s_aux, r_aux, s_el, r_el, s_er, r_er, s1, r1, s2, r2,
 ):
     lat, lon = lax.axis_index("lat"), lax.axis_index("lon")
-    band, lanes = depth_ref.shape
+    band, lanes = depth_hbm.shape
     groups = rank // T
     slot = lanes // groups
     half_slot = slot // 2
@@ -71,8 +80,20 @@
         pl.semaphore_signal(barrier, inc=1, device_id=at(a, b), device_id_type=MESH)
 
     has_up, has_dn = lat > 0, lat < n_lat - 1
-    aux[0 : 3 * band, :] = mean_ref[...]
-    aux[3 * band :, :] = depth_ref[...]
+    fetched = [
+        pltpu.make_async_copy(src, dst, s_in.at[i])
+        for i, (src, dst) in enumerate((
+            (mean_hbm, aux.at[pl.ds(0, 3 * band)]),
+            (depth_hbm, aux.at[pl.ds(3 * band, band)]),
+            (fac_hbm, fac_ref),
+            (cells_hbm, cells_ref),
+            (count_hbm, count_ref),
+            (vals_hbm, vals_ref),
+            (err_hbm, err_ref),
+        ))
+    ]
+    for copy in fetched:
+        copy.start()
 
     @pl.when(jnp.logical_not(has_up))
     def _():
@@ -96,7 +117,7 @@
     def main_copy(side, g):
         rows = pl.ds(g * chunk, chunk)
         dst = (up_buf, dn_buf)[side]
-        return remote(fac_ref.at[rows], dst.at[rows], s_main.at[side, g], r_main.at[side, g], at(1 - 2 * side, 0))
+        return remote(fac_hbm.at[rows], dst.at[rows], s_main.at[side, g], r_main.at[side, g], at(1 - 2 * side, 0))
 
     def aux_copy(side):
         dst = (aux_up, aux_dn)[side]
@@ -112,6 +133,8 @@
     receives = (has_up, has_dn)
 
     pl.semaphore_wait(barrier, len(peers))
+    fetched[0].wait()
+    fetched[1].wait()
     for side in range(2):
         @pl.when(sends[side])
         def _(side=side):
@@ -135,6 +158,7 @@
             )
         return tiles
 
+    fetched[2].wait()
     fold = slot // edge
     own_seams = []
     tiles_per = band // fold
@@ -171,6 +195,8 @@
         else:
             pl.when(sends[0] if block == 0 else sends[1])(go)
 
+    for copy in fetched[3:]:
+        copy.wait()
     cells = cells_ref[...]
     slots = cells.shape[1]
     live = lax.broadcasted_iota(jnp.int32, (1, slots), 1) < count_ref[...]
@@ -181,12 +207,15 @@
         obs_row = obs_row + jnp.where(cells >= r * lanes, 1, 0)
     obs_col = cells - lanes * obs_row
     row_hot = lax.broadcasted_iota(jnp.int32, (band, slots), 0) == obs_row
-    left_side = jnp.concatenate(
+    sums = jnp.concatenate(
         [jnp.where(row_hot, square, 0.0), jnp.where(row_hot, square * vals_ref[...], 0.0)], 0
     )
     col_hot = jnp.where(lax.broadcasted_iota(jnp.int32, (lanes, slots), 0) == obs_col, 1.0, 0.0)
-    cell_sums = lax.dot_general(left_side, col_hot, NT, precision=HIGHEST, preferred_element_type=jnp.float32)
-    cell_weight, cell_value = cell_sums[:band], cell_sums[band:]
+    sums = lax.dot_general(
+        jnp.concatenate(split(sums, 3), 0), col_hot.astype(jnp.bfloat16), NT, preferred_element_type=jnp.float32
+    )
+    sums = (sums[4 * band :] + sums[2 * band : 4 * band]) + sums[: 2 * band]
+    cell_weight, cell_value = sums[:band], sums[band:]
 
     half = 0.5 * TIME_STEP
     up_gain = jnp.where(has_up, half, 0.0).astype(jnp.float32)
@@ -286,21 +315,28 @@
                 spot = (f * band + r, slice(T * g, T * (g + 1)), slice(None))
                 fc[spot] = jnp.where(at_edge, back[T * r : T * (r + 1)], fc[spot])
 
+    for f in range(3):
+        for r in range(band):
+            mean_out[f * band + r : f * band + r + 1, :] = mean[f][T * r : T * r + 1]
+
     lhs, rhs = [], []
     for r in range(band):
         height = fc[r]
         w = cell_weight[r : r + 1]
         drive = cell_value[r : r + 1] - w * mean[0][T * r : T * r + 1]
         lhs.append(height)
-        rhs.append(jnp.concatenate([height * w, jnp.where(sub8 == 0, drive, 0.0)], 0))
+        pad = jnp.zeros((lanes // 2 - rank - T, lanes), jnp.float32)
+        rhs.append(jnp.concatenate([height * w, jnp.where(sub8 == 0, drive, 0.0), pad], 0))
     gram = lax.dot_general(
-        jnp.concatenate(lhs, 1), jnp.concatenate(rhs, 1), NT, precision=HIGHEST, preferred_element_type=jnp.float32
+        jnp.concatenate(split(jnp.concatenate(lhs, 1), 2), 0),
+        jnp.concatenate(split(jnp.concatenate(rhs, 1), 2), 0),
+        NT, preferred_element_type=jnp.float32,
     )
-    gt[...] = jnp.zeros_like(gt)
-    gt[:, 0 : rank + T] = gram
+    gram = gram[:rank] + gram[rank:]
+    gram = gram + roll(gram, lanes // 2)
     hr = rank // 2
     wide = lax.broadcasted_iota(jnp.int32, (hr, lanes), 1)
-    mine = jnp.where(wide < lanes // 2, gt[0:hr, :], roll(gt[hr:, :], lanes // 2))
+    mine = jnp.where(wide < lanes // 2, gram[:hr], gram[hr:])
 
     p1[...] = mine
     def lat_copy(o):
@@ -319,41 +355,7 @@
         lon_copy(o).wait_recv()
         mine = mine + ar2[o - 1]
 
-    both = jnp.concatenate([mine, roll(mine, lanes // 2)], 0)
-    ri = lax.broadcasted_iota(jnp.int32, (rank, lanes), 0)
-    li = lax.broadcasted_iota(jnp.int32, (rank, lanes), 1)
-    eyes = jnp.where((li == ri) | (li == ri + lanes // 2), 1.0, 0.0)
-    x = jnp.where(li < lanes // 2, both, 0.0) + eyes
-    tiles = [x[T * i : T * (i + 1)] for i in range(groups)]
-    for j in range(rank):
-        tj, sj = j // T, j % T
-        row = tiles[tj][sj : sj + 1]
-        inv = 1.0 / row[:, j : j + 1]
-        scaled_row = row * inv
-        for i in range(tj, groups):
-            if i == tj and sj == T - 1:
-                continue
-            col = tiles[i][:, j : j + 1]
-            if i == tj:
-                col = jnp.where(sub8[:, :1] > sj, col, 0.0)
-            tiles[i] = tiles[i] - col * scaled_row
-    x = jnp.concatenate(tiles, 0)
-    pivot = jnp.sum(jnp.where(li == ri, x, 0.0), 1, keepdims=True)
-    x = x / jnp.sqrt(pivot)
-    inverse = jnp.where(li < rank, roll(x, -(lanes // 2)), 0.0)
-    z = x[:, rank : rank + 1]
-    shift = jnp.sum(inverse * z, 0, keepdims=True)
-    coefs = jnp.concatenate([inverse, jnp.where(sub8 == 0, shift, 0.0)], 0)[:, :rank]
-
-    for f in range(3):
-        slab = jnp.concatenate([fc[f * band + r] for r in range(band)], 1)
-        res = jnp.dot(coefs, slab, precision=HIGHEST, preferred_element_type=jnp.float32)
-        for r in range(band):
-            part = res[:, lanes * r : lanes * (r + 1)]
-            i = f * band + r
-            for g in range(groups):
-                out_ref[pl.ds(g * chunk + i, T, stride=per), :] = part[T * g : T * (g + 1)]
-            upd_ref[i : i + 1, :] = mean[f][T * r : T * r + 1] + part[rank : rank + 1]
+    gram_out[...] = mine
 
     for side in range(2):
         @pl.when(sends[side])
@@ -371,6 +373,72 @@
         lon_copy(o).wait_send()
 
 
+def transform(rank, fc, mean_ref, gram_ref, upd_hbm, out_hbm, upd, res, s_out):
+    mine = gram_ref[...]
+    lanes = mine.shape[1]
+    band = fc.shape[0] // 3
+    groups = rank // T
+    sub8 = lax.broadcasted_iota(jnp.int32, (T, lanes), 0)
+    both = jnp.concatenate([mine, roll(mine, lanes // 2)], 0)
+    ri = lax.broadcasted_iota(jnp.int32, (rank, lanes), 0)
+    li = lax.broadcasted_iota(jnp.int32, (rank, lanes), 1)
+    eyes = jnp.where((li == ri) | (li == ri + lanes // 2), 1.0, 0.0)
+    x = jnp.where(li < lanes // 2, both, 0.0) + eyes
+    tiles = [x[T * i : T * (i + 1)] for i in range(groups)]
+    for b in range(groups):
+        cols = {
+            (i, q): jnp.broadcast_to(tiles[i][:, T * b + q : T * b + q + 1], (T, lanes))
+            for i in range(b, groups)
+            for q in range(T)
+        }
+        for q in range(T):
+            inv = 1.0 / cols[b, q][q : q + 1]
+            row = tiles[b][q : q + 1]
+            heads = [cols[b, p][q : q + 1] for p in range(q + 1, T)]
+            for i in range(b, groups):
+                if i == b and q == T - 1:
+                    continue
+                m = cols[i, q] * inv
+                if i == b:
+                    m = jnp.where(sub8 > q, m, 0.0)
+                for p in range(q + 1, T):
+                    cols[i, p] = cols[i, p] - m * heads[p - q - 1]
+                tiles[i] = tiles[i] - m * row
+    x = jnp.concatenate(tiles, 0)
+    pivot = jnp.sum(jnp.where(li == ri, x, 0.0), 1, keepdims=True)
+    x = x / jnp.sqrt(pivot)
+    inverse = jnp.where(li < rank, roll(x, -(lanes // 2)), 0.0)
+    z = x[:, rank : rank + 1]
+    shift = jnp.sum(inverse * z, 0, keepdims=True)
+    coefs = jnp.concatenate([inverse, jnp.where(sub8 == 0, shift, 0.0)], 0)
+    high, low = (c.astype(jnp.float32) for c in split(coefs, 2))
+    stacked = (high + roll(high, rank) + roll(low, 2 * rank))[:, : 3 * rank].astype(jnp.bfloat16)
+
+    per = 3 * band
+    for f in range(3):
+        slab = jnp.concatenate([fc[f * band + r] for r in range(band)], 1)
+        high, low = split(slab, 2)
+        part = jnp.dot(stacked, jnp.concatenate([high, low, high], 0), preferred_element_type=jnp.float32)
+        for r in range(band):
+            col = part[:, lanes * r : lanes * (r + 1)]
+            i = f * band + r
+            for g in range(groups):
+                res[pl.ds(g * T * per + i, T, stride=per), :] = col[T * g : T * (g + 1)]
+            upd[i : i + 1, :] = mean_ref[i : i + 1, :] + col[rank : rank + 1]
+    copies = [
+        pltpu.make_async_copy(res, out_hbm, s_out.at[0]),
+        pltpu.make_async_copy(upd, upd_hbm, s_out.at[1]),
+    ]
+    for copy in copies:
+        copy.start()
+    for copy in copies:
+        copy.wait()
+
+
+def in_hbm(x):
+    return pltpu.with_memory_space_constraint(x, pltpu.HBM)
+
+
 def per_device(n_lat, n_lon, background, factor, depth, cells, count, values, error):
     rank, fields, band, lanes = factor.shape
     groups = rank // T
@@ -381,20 +449,23 @@
     vmem = pl.BlockSpec(memory_space=pltpu.VMEM)
     f32 = functools.partial(pltpu.VMEM, dtype=jnp.float32)
     dma = pltpu.SemaphoreType.DMA
-    updated, analysis = pl.pallas_call(
+    anywhere = pl.BlockSpec(memory_space=pl.ANY)
+    forecast, mean, gram = pl.pallas_call(
         functools.partial(kernel, n_lat, n_lon, rank),
         out_shape=(
+            jax.ShapeDtypeStruct((fields * band, rank, lanes), jnp.float32),
             jax.ShapeDtypeStruct((fields * band, lanes), jnp.float32),
-            jax.ShapeDtypeStruct((rows, lanes), jnp.float32),
+            jax.ShapeDtypeStruct((rank // 2, lanes), jnp.float32),
         ),
-        in_specs=[vmem] * 7,
-        out_specs=(vmem, vmem),
+        in_specs=[pl.BlockSpec(memory_space=pltpu.HBM)] * 7,
+        out_specs=(vmem, vmem, vmem),
         scratch_shapes=[
+            f32((rows, lanes)), pltpu.VMEM((1, slots), jnp.int32), pltpu.VMEM((1, 1), jnp.int32),
+            f32((1, slots)), f32((1, slots)), dma((7,)),
             f32((rows, lanes)), f32((rows, lanes)),
             f32((4 * band, lanes)), f32((4 * band, lanes)), f32((4 * band, lanes)),
             f32((edge_rows, lanes)), f32((edge_rows, lanes)),
             f32((3, edge_rows, lanes)), f32((3, edge_rows, lanes)),
-            f32((fields * band, rank, lanes)), f32((rank, lanes)),
             f32((rank // 2, lanes)), f32((rank // 2, lanes)),
             f32((n_lat - 1, rank // 2, lanes)), f32((n_lon - 1, rank // 2, lanes)),
             dma((2, groups)), dma((2, groups)), dma((2,)), dma((2,)),
@@ -405,9 +476,20 @@
             collective_id=0, has_side_effects=True, vmem_limit_bytes=32 * 1024 * 1024
         ),
     )(
-        background.reshape(fields * band, lanes), factor.reshape(rows, lanes), depth,
-        cells.reshape(1, slots), count.reshape(1, 1), values.reshape(1, slots), error.reshape(1, slots),
+        in_hbm(background.reshape(fields * band, lanes)), in_hbm(factor.reshape(rows, lanes)), in_hbm(depth),
+        in_hbm(cells.reshape(1, slots)), count.reshape(1, 1), in_hbm(values.reshape(1, slots)), in_hbm(error.reshape(1, slots)),
     )
+    updated, analysis = pl.pallas_call(
+        functools.partial(transform, rank),
+        out_shape=(
+            jax.ShapeDtypeStruct((fields * band, lanes), jnp.float32),
+            jax.ShapeDtypeStruct((rows, lanes), jnp.float32),
+        ),
+        in_specs=[vmem] * 3,
+        out_specs=(anywhere, anywhere),
+        scratch_shapes=[f32((fields * band, lanes)), f32((rows, lanes)), dma((2,))],
+        compiler_params=pltpu.CompilerParams(vmem_limit_bytes=16 * 1024 * 1024),
+    )(forecast, mean, gram)
     return updated.reshape(background.shape), analysis.reshape(factor.shape)
 
 

time: 32.4 us -> 26 us (0.80)
  local copies, waits for them, and re-layouts: 5.06 us -> 0 us
  Pallas kernels: 25.7 us -> 24.6 us
    unnamed x14 -> x0, local copies, waits for them, and re-layouts: 5.06 us -> none
    pallas_call x1, Pallas kernels: 25.7 us -> 22.6 us  [per_device(): pl.pallas_call(functools.partial(kernel, n_lat, n_lon, rank), out_shape=(...]
    pallas_call x0 -> x1, Pallas kernels: none -> 1.96 us  [per_device(): pl.pallas_call(functools.partial(transform, rank), out_shape=(jax.ShapeDt...]
where the time goes in v2:
time: 26 us; the launch traced here: 25.8 us
  Pallas kernels  24.6 us (95%)
  between operations  1.29 us (5%)
    pallas_call x1, Pallas kernels, per_device(): pl.pallas_call(functools.partial(kernel, n_lat, n_lon, rank), out_shape=(...  22.6 us
    pallas_call x1, Pallas kernels, per_device(): pl.pallas_call(functools.partial(transform, rank), out_shape=(jax.ShapeDt...  1.96 us

profile of v2, /device:TPU:0, one launch (start us, length us, event | category | flops | bytes accessed | tf_op | source)
XLA Modules:
  0.0 25.8 jit_solution(3560238788547259464)
XLA Ops:
  1.3 22.6 %shard_map.86 = (f32[24,32,128]{2,1,0:T(8,128)S(1)}, f32[24,128]{1,0:T(8,128)S(1)}, f32[16,128]{1,0:T(8,128)S(1)}) custom-call(f32[24,128]{1,0:T(8,128)} %bitcast.10, f32[768,128]{1,0:T(8,128)} %bitcast.9, f32[8,128]{1,0:T(8,128)} %depth_hbm.1, s32[1,256]{1,0:T(1,128)} %bitcast.11, s32[1,1]{1,0:T(1,128)} %bitcast.8.count_hbm, f32[1,256]{1,0:T(1,128)} %bitcast.12, ...), custom_call_target="tpu_custom_call" | custom-call | tf_op jit(solution)/shard_map/pallas_call | solution.py:453
  23.9 2.0 %shard_map.87 = (f32[24,128]{1,0:T(8,128)}, f32[768,128]{1,0:T(8,128)}) custom-call(f32[24,32,128]{2,1,0:T(8,128)S(1)} %get-tuple-element.7.fc, f32[24,128]{1,0:T(8,128)S(1)} %get-tuple-element.8.mean_ref, f32[16,128]{1,0:T(8,128)S(1)} %get-tuple-element.9.gram_ref), custom_call_target="tpu_custom_call" | custom-call | tf_op jit(solution)/shard_map/pallas_call | solution.py:482

commit v3 on v2

--- a/solution.py
+++ b/solution.py
@@ -56,7 +56,7 @@
     fc, mean_out, gram_out,
     fac_ref, cells_ref, count_ref, vals_ref, err_ref, s_in,
     up_buf, dn_buf, aux, aux_up, aux_dn, edge_right, edge_left, from_left, from_right,
-    p1, p2, ar1, ar2,
+    seam_buf, p1, p2, ar1, ar2,
     s_main, r_main, s_aux, r_aux, s_el, r_el, s_er, r_er, s1, r1, s2, r2,
 ):
     lat, lon = lax.axis_index("lat"), lax.axis_index("lon")
@@ -135,12 +135,20 @@
     pl.semaphore_wait(barrier, len(peers))
     fetched[0].wait()
     fetched[1].wait()
+
+    def send_group(g):
+        for side in range(2):
+            @pl.when(sends[side])
+            def _(side=side):
+                main_copy(side, g).start()
+
     for side in range(2):
         @pl.when(sends[side])
         def _(side=side):
             aux_copy(side).start()
-            for g in range(groups):
-                main_copy(side, g).start()
+    early = groups // 2
+    for g in range(early):
+        send_group(g)
 
     def load(ref, f, g):
         return jnp.concatenate([ref[pl.ds(g * chunk + f * band + r, T, stride=per), :] for r in range(band)], 0)
@@ -194,6 +202,8 @@
             go()
         else:
             pl.when(sends[0] if block == 0 else sends[1])(go)
+    for g in range(early, groups):
+        send_group(g)
 
     for copy in fetched[3:]:
         copy.wait()
@@ -232,16 +242,29 @@
     coef = jnp.concatenate([half * spread(b[3 * band :, :]) for b in aux_blocks], 0)
 
     blocks = (up_buf, fac_ref, dn_buf)
-    for g in range(groups):
+
+    def take_group(g):
         for side in range(2):
             @pl.when(receives[side])
-            def _(side=side, g=g):
+            def _(side=side):
                 main_copy(side, g).wait_recv()
-        state = [jnp.concatenate([load(b, f, g) for b in blocks], 0) for f in range(3)]
+        state = []
+        for f in range(3):
+            loaded = [load(b, f, g) for b in blocks]
+            state.append(jnp.concatenate(loaded, 0))
+            for side in range(2):
+                spot = (side * 3 + f,)
+                tiles = roll(loaded[2 * side], slot * g + half_slot)
+                if g > 0:
+                    tiles = jnp.where(stack_lane >= slot * g, tiles, seam_buf[spot])
+                seam_buf[spot] = tiles
         state = evolve(*state, coef, up_gain, down_gain, band)
         for f in range(3):
             for r in range(band):
                 fc[f * band + r, T * g : T * (g + 1), :] = state[f][T * r : T * (r + 1)]
+
+    for g in range(early):
+        take_group(g)
 
     edge_copy(True, 1).wait_recv()
     edge_copy(False, 1).wait_recv()
@@ -287,6 +310,9 @@
     coef_left = jnp.concatenate([half * spread(repeat_slots(s)) for s in strips_of], 0)
     coef_right = jnp.concatenate([half * spread(repeat_slots(roll(s, -slot))) for s in strips_of], 0)
 
+    for g in range(early, groups):
+        take_group(g)
+
     def unpack(ref, b, f, first):
         out = []
         for r in range(band):
@@ -299,7 +325,7 @@
     for f in range(3):
         lefts, rights = [], []
         for b in range(3):
-            seams = own_seams[f] if b == 1 else seam_tiles(blocks[b], f)
+            seams = own_seams[f] if b == 1 else seam_buf[(b // 2) * 3 + f]
             lefts.append(jnp.where(low_half, unpack(from_left, b, f, half_slot - edge), seams))
             rights.append(jnp.where(low_half, seams, unpack(from_right, b, f, half_slot)))
         left_state.append(jnp.concatenate(lefts, 0))
@@ -307,7 +333,8 @@
     left_state = evolve(*left_state, coef_left, up_gain, down_gain, band)
     right_state = evolve(*right_state, coef_right, up_gain, down_gain, band)
     at_edge = (lane8 < edge) | (lane8 >= lanes - edge)
-    for f in range(3):
+
+    def merge(f):
         seams = jnp.where(low_half, right_state[f], left_state[f])
         for g in range(groups):
             back = roll(seams, -(slot * g + half_slot))
@@ -315,10 +342,7 @@
                 spot = (f * band + r, slice(T * g, T * (g + 1)), slice(None))
                 fc[spot] = jnp.where(at_edge, back[T * r : T * (r + 1)], fc[spot])
 
-    for f in range(3):
-        for r in range(band):
-            mean_out[f * band + r : f * band + r + 1, :] = mean[f][T * r : T * r + 1]
-
+    merge(0)
     lhs, rhs = [], []
     for r in range(band):
         height = fc[r]
@@ -345,6 +369,11 @@
         return remote(p2, ar2.at[o - 1], s2.at[o - 1], r2.at[o - 1], at(0, o))
     for o in range(1, n_lat):
         lat_copy(o).start()
+    merge(1)
+    merge(2)
+    for f in range(3):
+        for r in range(band):
+            mean_out[f * band + r : f * band + r + 1, :] = mean[f][T * r : T * r + 1]
     for o in range(1, n_lat):
         lat_copy(o).wait_recv()
         mine = mine + ar1[o - 1]
@@ -466,7 +495,7 @@
             f32((4 * band, lanes)), f32((4 * band, lanes)), f32((4 * band, lanes)),
             f32((edge_rows, lanes)), f32((edge_rows, lanes)),
             f32((3, edge_rows, lanes)), f32((3, edge_rows, lanes)),
-            f32((rank // 2, lanes)), f32((rank // 2, lanes)),
+            f32((2 * fields, T * band, lanes)), f32((rank // 2, lanes)), f32((rank // 2, lanes)),
             f32((n_lat - 1, rank // 2, lanes)), f32((n_lon - 1, rank // 2, lanes)),
             dma((2, groups)), dma((2, groups)), dma((2,)), dma((2,)),
             dma((3,)), dma((3,)), dma((3,)), dma((3,)),

time: 26 us -> 26.1 us (level)
  no operation moved by 1% of the time
where the time goes in v3:
time: 26.1 us; the launch traced here: 25.9 us
  Pallas kernels  24.7 us (95%)
  between operations  1.29 us (5%)
    pallas_call x1, Pallas kernels, per_device(): pl.pallas_call(functools.partial(kernel, n_lat, n_lon, rank), out_shape=(...  22.7 us
    pallas_call x1, Pallas kernels, per_device(): pl.pallas_call(functools.partial(transform, rank), out_shape=(jax.ShapeDt...  1.96 us

profile of v3, /device:TPU:0, one launch (start us, length us, event | category | flops | bytes accessed | tf_op | source)
XLA Modules:
  0.0 25.9 jit_solution(2694257667981437006)
XLA Ops:
  1.3 22.7 %shard_map.86 = (f32[24,32,128]{2,1,0:T(8,128)S(1)}, f32[24,128]{1,0:T(8,128)S(1)}, f32[16,128]{1,0:T(8,128)S(1)}) custom-call(f32[24,128]{1,0:T(8,128)} %bitcast.10, f32[768,128]{1,0:T(8,128)} %bitcast.9, f32[8,128]{1,0:T(8,128)} %depth_hbm.1, s32[1,256]{1,0:T(1,128)} %bitcast.11, s32[1,1]{1,0:T(1,128)} %bitcast.8.count_hbm, f32[1,256]{1,0:T(1,128)} %bitcast.12, ...), custom_call_target="tpu_custom_call" | custom-call | tf_op jit(solution)/shard_map/pallas_call | solution.py:482
  24.0 2.0 %shard_map.87 = (f32[24,128]{1,0:T(8,128)}, f32[768,128]{1,0:T(8,128)}) custom-call(f32[24,32,128]{2,1,0:T(8,128)S(1)} %get-tuple-element.7.fc, f32[24,128]{1,0:T(8,128)S(1)} %get-tuple-element.8.mean_ref, f32[16,128]{1,0:T(8,128)S(1)} %get-tuple-element.9.gram_ref), custom_call_target="tpu_custom_call" | custom-call | tf_op jit(solution)/shard_map/pallas_call | solution.py:511

commit v4 on v3

--- a/solution.py
+++ b/solution.py
@@ -56,7 +56,7 @@
     fc, mean_out, gram_out,
     fac_ref, cells_ref, count_ref, vals_ref, err_ref, s_in,
     up_buf, dn_buf, aux, aux_up, aux_dn, edge_right, edge_left, from_left, from_right,
-    seam_buf, p1, p2, ar1, ar2,
+    seam_buf, own_seams, coef_buf, strip_state, strip_out, p1, p2, ar1, ar2,
     s_main, r_main, s_aux, r_aux, s_el, r_el, s_er, r_er, s1, r1, s2, r2,
 ):
     lat, lon = lax.axis_index("lat"), lax.axis_index("lon")
@@ -168,12 +168,12 @@
 
     fetched[2].wait()
     fold = slot // edge
-    own_seams = []
     tiles_per = band // fold
     in_slot = lax.rem(lane8, slot)
-    for f in range(3):
+
+    def pack(f, carry):
         seams = seam_tiles(fac_ref, f)
-        own_seams.append(seams)
+        own_seams[f] = seams
         for t in range(tiles_per):
             right = left = None
             for q in range(fold):
@@ -183,9 +183,12 @@
                 keep = (in_slot >= edge * q) & (in_slot < edge * (q + 1))
                 right = to_right if q == 0 else jnp.where(keep, to_right, right)
                 left = to_left if q == 0 else jnp.where(keep, to_left, left)
-            row = T * (f * tiles_per + t)
-            edge_right[row : row + T, :] = right
-            edge_left[row : row + T, :] = left
+            row = pl.ds(pl.multiple_of(T * (f * tiles_per + t), T), T)
+            edge_right[row, :] = right
+            edge_left[row, :] = left
+        return carry
+
+    lax.fori_loop(0, 3, pack, 0)
     aux_edge = None
     for f in range(4):
         tile = roll(aux[f * band : (f + 1) * band, :], 2 * edge * f + edge)
@@ -239,11 +242,13 @@
         def _(side=side):
             aux_copy(side).wait_recv()
     aux_blocks = (aux_up, aux, aux_dn)
-    coef = jnp.concatenate([half * spread(b[3 * band :, :]) for b in aux_blocks], 0)
+    for b in range(3):
+        coef_buf[3, T * band * b : T * band * (b + 1), :] = half * spread(aux_blocks[b][3 * band :, :])
+    seam_buf[...] = jnp.zeros_like(seam_buf)
 
     blocks = (up_buf, fac_ref, dn_buf)
 
-    def take_group(g):
+    def take_group(g, carry):
         for side in range(2):
             @pl.when(receives[side])
             def _(side=side):
@@ -254,17 +259,16 @@
             state.append(jnp.concatenate(loaded, 0))
             for side in range(2):
                 spot = (side * 3 + f,)
-                tiles = roll(loaded[2 * side], slot * g + half_slot)
-                if g > 0:
-                    tiles = jnp.where(stack_lane >= slot * g, tiles, seam_buf[spot])
-                seam_buf[spot] = tiles
-        state = evolve(*state, coef, up_gain, down_gain, band)
+                tiles = pltpu.roll(loaded[2 * side], slot * g + half_slot, 1)
+                seam_buf[spot] = jnp.where(stack_lane >= slot * g, tiles, seam_buf[spot])
+        state = evolve(*state, coef_buf[3], up_gain, down_gain, band)
+        spot = pl.ds(pl.multiple_of(T * g, T), T)
         for f in range(3):
             for r in range(band):
-                fc[f * band + r, T * g : T * (g + 1), :] = state[f][T * r : T * (r + 1)]
-
-    for g in range(early):
-        take_group(g)
+                fc[f * band + r, spot, :] = state[f][T * r : T * (r + 1)]
+        return carry
+
+    lax.fori_loop(0, groups, take_group, 0)
 
     edge_copy(True, 1).wait_recv()
     edge_copy(False, 1).wait_recv()
@@ -290,15 +294,6 @@
         own, strips = aux_pair(b, f)
         return jnp.concatenate([jnp.where(sub8 == 0, own[r : r + 1], strips[r : r + 1]) for r in range(band)], 0)
 
-    mean_state = [jnp.concatenate([mean_group(b, f) for b in range(3)], 0) for f in range(4)]
-    mean_state = evolve(*mean_state[:3], half * mean_state[3], up_gain, down_gain, band)
-    mean = []
-    for f in range(3):
-        strips = roll(mean_state[f], -1, 0)
-        low = roll(strips, -half_slot)
-        high = roll(strips, lanes - half_slot - slot)
-        mean.append(jnp.where(stack_lane < edge, low, jnp.where(stack_lane >= lanes - edge, high, mean_state[f])))
-
     def repeat_slots(tile):
         tile = jnp.where(lane8 < slot, tile, 0.0)
         total = tile
@@ -307,40 +302,60 @@
         return total
 
     strips_of = [aux_pair(b, 3)[1] for b in range(3)]
-    coef_left = jnp.concatenate([half * spread(repeat_slots(s)) for s in strips_of], 0)
-    coef_right = jnp.concatenate([half * spread(repeat_slots(roll(s, -slot))) for s in strips_of], 0)
-
-    for g in range(early, groups):
-        take_group(g)
+    for b in range(3):
+        rows = slice(T * band * b, T * band * (b + 1))
+        coef_buf[0, rows, :] = half * spread(repeat_slots(strips_of[b]))
+        coef_buf[1, rows, :] = half * spread(repeat_slots(roll(strips_of[b], -slot)))
+        coef_buf[2, rows, :] = half * mean_group(b, 3)
+        for f in range(3):
+            strip_state[2, f, rows, :] = mean_group(b, f)
 
     def unpack(ref, b, f, first):
         out = []
         for r in range(band):
-            row = T * (f * tiles_per + r // fold)
-            out.append(roll(ref[b, row : row + T, :], first - edge * (r % fold)))
+            row = pl.ds(pl.multiple_of(T * (f * tiles_per + r // fold), T), T)
+            out.append(roll(ref[b, row, :], first - edge * (r % fold)))
         return jnp.concatenate(out, 0)
 
     low_half = lax.rem(stack_lane, slot) < half_slot
-    left_state, right_state = [], []
+
+    def join(f, carry):
+        for b in range(3):
+            rows = slice(T * band * b, T * band * (b + 1))
+            seams = own_seams[f] if b == 1 else seam_buf[(b // 2) * 3 + f]
+            strip_state[0, f, rows, :] = jnp.where(low_half, unpack(from_left, b, f, half_slot - edge), seams)
+            strip_state[1, f, rows, :] = jnp.where(low_half, seams, unpack(from_right, b, f, half_slot))
+        return carry
+
+    lax.fori_loop(0, 3, join, 0)
+
+    def take_strips(u, carry):
+        state = evolve(*(strip_state[u, f] for f in range(3)), coef_buf[u], up_gain, down_gain, band)
+        for f in range(3):
+            strip_out[u, f] = state[f]
+        return carry
+
+    lax.fori_loop(0, 3, take_strips, 0)
+    mean = []
     for f in range(3):
-        lefts, rights = [], []
-        for b in range(3):
-            seams = own_seams[f] if b == 1 else seam_buf[(b // 2) * 3 + f]
-            lefts.append(jnp.where(low_half, unpack(from_left, b, f, half_slot - edge), seams))
-            rights.append(jnp.where(low_half, seams, unpack(from_right, b, f, half_slot)))
-        left_state.append(jnp.concatenate(lefts, 0))
-        right_state.append(jnp.concatenate(rights, 0))
-    left_state = evolve(*left_state, coef_left, up_gain, down_gain, band)
-    right_state = evolve(*right_state, coef_right, up_gain, down_gain, band)
+        whole = strip_out[2, f]
+        strips = roll(whole, -1, 0)
+        low = roll(strips, -half_slot)
+        high = roll(strips, lanes - half_slot - slot)
+        mean.append(jnp.where(stack_lane < edge, low, jnp.where(stack_lane >= lanes - edge, high, whole)))
     at_edge = (lane8 < edge) | (lane8 >= lanes - edge)
 
     def merge(f):
-        seams = jnp.where(low_half, right_state[f], left_state[f])
-        for g in range(groups):
-            back = roll(seams, -(slot * g + half_slot))
+        seams = jnp.where(low_half, strip_out[1, f], strip_out[0, f])
+
+        def one(g, carry):
+            back = pltpu.roll(seams, lanes - (slot * g + half_slot), 1)
             for r in range(band):
-                spot = (f * band + r, slice(T * g, T * (g + 1)), slice(None))
+                spot = (f * band + r, pl.ds(pl.multiple_of(T * g, T), T), slice(None))
                 fc[spot] = jnp.where(at_edge, back[T * r : T * (r + 1)], fc[spot])
+            return carry
+
+        lax.fori_loop(0, groups, one, 0)
 
     merge(0)
     lhs, rhs = [], []
@@ -495,7 +510,8 @@
             f32((4 * band, lanes)), f32((4 * band, lanes)), f32((4 * band, lanes)),
             f32((edge_rows, lanes)), f32((edge_rows, lanes)),
             f32((3, edge_rows, lanes)), f32((3, edge_rows, lanes)),
-            f32((2 * fields, T * band, lanes)), f32((rank // 2, lanes)), f32((rank // 2, lanes)),
+            f32((2 * fields, T * band, lanes)), f32((fields, T * band, lanes)), f32((4, 3 * T * band, lanes)),
+            f32((3, fields, 3 * T * band, lanes)), f32((3, fields, T * band, lanes)), f32((rank // 2, lanes)), f32((rank // 2, lanes)),
             f32((n_lat - 1, rank // 2, lanes)), f32((n_lon - 1, rank // 2, lanes)),
             dma((2, groups)), dma((2, groups)), dma((2,)), dma((2,)),
             dma((3,)), dma((3,)), dma((3,)), dma((3,)),

time: 26.1 us -> 26.9 us (1.031)
  Pallas kernels: 24.7 us -> 25.5 us
    pallas_call x1, Pallas kernels: 22.7 us -> 23.5 us  [per_device(): pl.pallas_call(functools.partial(kernel, n_lat, n_lon, rank), out_shape=(...]
where the time goes in v4:
time: 26.9 us; the launch traced here: 26.8 us
  Pallas kernels  25.5 us (95%)
  between operations  1.29 us (5%)
    pallas_call x1, Pallas kernels, per_device(): pl.pallas_call(functools.partial(kernel, n_lat, n_lon, rank), out_shape=(...  23.5 us
    pallas_call x1, Pallas kernels, per_device(): pl.pallas_call(functools.partial(transform, rank), out_shape=(jax.ShapeDt...  1.96 us

profile of v4, /device:TPU:0, one launch (start us, length us, event | category | flops | bytes accessed | tf_op | source)
XLA Modules:
  0.0 26.8 jit_solution(4290438128804999479)
XLA Ops:
  1.3 23.5 %shard_map.86 = (f32[24,32,128]{2,1,0:T(8,128)S(1)}, f32[24,128]{1,0:T(8,128)S(1)}, f32[16,128]{1,0:T(8,128)S(1)}) custom-call(f32[24,128]{1,0:T(8,128)} %bitcast.10, f32[768,128]{1,0:T(8,128)} %bitcast.9, f32[8,128]{1,0:T(8,128)} %depth_hbm.1, s32[1,256]{1,0:T(1,128)} %bitcast.11, s32[1,1]{1,0:T(1,128)} %bitcast.8.count_hbm, f32[1,256]{1,0:T(1,128)} %bitcast.12, ...), custom_call_target="tpu_custom_call" | custom-call | tf_op jit(solution)/shard_map/pallas_call | solution.py:497
  24.8 2.0 %shard_map.87 = (f32[24,128]{1,0:T(8,128)}, f32[768,128]{1,0:T(8,128)}) custom-call(f32[24,32,128]{2,1,0:T(8,128)S(1)} %get-tuple-element.7.fc, f32[24,128]{1,0:T(8,128)S(1)} %get-tuple-element.8.mean_ref, f32[16,128]{1,0:T(8,128)S(1)} %get-tuple-element.9.gram_ref), custom_call_target="tpu_custom_call" | custom-call | tf_op jit(solution)/shard_map/pallas_call | solution.py:527

commit v5 on v3

--- a/solution.py
+++ b/solution.py
@@ -56,8 +56,8 @@
     fc, mean_out, gram_out,
     fac_ref, cells_ref, count_ref, vals_ref, err_ref, s_in,
     up_buf, dn_buf, aux, aux_up, aux_dn, edge_right, edge_left, from_left, from_right,
-    seam_buf, p1, p2, ar1, ar2,
-    s_main, r_main, s_aux, r_aux, s_el, r_el, s_er, r_er, s1, r1, s2, r2,
+    seam_buf,
+    s_main, r_main, s_aux, r_aux, s_el, r_el, s_er, r_er,
 ):
     lat, lon = lax.axis_index("lat"), lax.axis_index("lon")
     band, lanes = depth_hbm.shape
@@ -74,7 +74,7 @@
         return (lax.rem(lat + dlat + n_lat, n_lat), lax.rem(lon + dlon + n_lon, n_lon))
 
     diagonals = [(a, b) for a in (-1, 1) for b in (-1, 1)]
-    peers = [(a, 0) for a in range(1, n_lat)] + [(0, b) for b in range(1, n_lon)] + diagonals
+    peers = [(-1, 0), (1, 0), (0, -1), (0, 1)] + diagonals
     barrier = pltpu.get_barrier_semaphore()
     for a, b in peers:
         pl.semaphore_signal(barrier, inc=1, device_id=at(a, b), device_id_type=MESH)
@@ -362,30 +362,12 @@
     wide = lax.broadcasted_iota(jnp.int32, (hr, lanes), 1)
     mine = jnp.where(wide < lanes // 2, gram[:hr], gram[hr:])
 
-    p1[...] = mine
-    def lat_copy(o):
-        return remote(p1, ar1.at[o - 1], s1.at[o - 1], r1.at[o - 1], at(o, 0))
-    def lon_copy(o):
-        return remote(p2, ar2.at[o - 1], s2.at[o - 1], r2.at[o - 1], at(0, o))
-    for o in range(1, n_lat):
-        lat_copy(o).start()
+    gram_out[...] = mine
     merge(1)
     merge(2)
     for f in range(3):
         for r in range(band):
             mean_out[f * band + r : f * band + r + 1, :] = mean[f][T * r : T * r + 1]
-    for o in range(1, n_lat):
-        lat_copy(o).wait_recv()
-        mine = mine + ar1[o - 1]
-    p2[...] = mine
-    for o in range(1, n_lon):
-        lon_copy(o).start()
-    for o in range(1, n_lon):
-        lon_copy(o).wait_recv()
-        mine = mine + ar2[o - 1]
-
-    gram_out[...] = mine
-
     for side in range(2):
         @pl.when(sends[side])
         def _(side=side):
@@ -396,10 +378,40 @@
             edge_copy(False, 2 * side).wait_send()
     edge_copy(True, 1).wait_send()
     edge_copy(False, 1).wait_send()
+
+def total(n_lat, n_lon, part_ref, sum_ref, mid, ar1, ar2, s1, r1, s2, r2):
+    lat, lon = lax.axis_index("lat"), lax.axis_index("lon")
+
+    def at(dlat, dlon):
+        return (lax.rem(lat + dlat, n_lat), lax.rem(lon + dlon, n_lon))
+
+    barrier = pltpu.get_barrier_semaphore()
     for o in range(1, n_lat):
-        lat_copy(o).wait_send()
+        pl.semaphore_signal(barrier, inc=1, device_id=at(o, 0), device_id_type=MESH)
     for o in range(1, n_lon):
-        lon_copy(o).wait_send()
+        pl.semaphore_signal(barrier, inc=1, device_id=at(0, o), device_id_type=MESH)
+    pl.semaphore_wait(barrier, n_lat + n_lon - 2)
+
+    def exchange(src, slots, ssem, rsem, count, step):
+        copies = [
+            pltpu.make_async_remote_copy(
+                src_ref=src, dst_ref=slots.at[o - 1], send_sem=ssem.at[o - 1], recv_sem=rsem.at[o - 1],
+                device_id=at(o * step[0], o * step[1]), device_id_type=MESH,
+            )
+            for o in range(1, count)
+        ]
+        for copy in copies:
+            copy.start()
+        mine = src[...]
+        for o, copy in enumerate(copies):
+            copy.wait_recv()
+            mine = mine + slots[o]
+        return mine, copies
+
+    mid[...], first = exchange(part_ref, ar1, s1, r1, n_lat, (1, 0))
+    sum_ref[...], second = exchange(mid, ar2, s2, r2, n_lon, (0, 1))
+    for copy in first + second:
+        copy.wait_send()
 
 
 def transform(rank, fc, mean_ref, gram_ref, upd_hbm, out_hbm, upd, res, s_out):
@@ -495,11 +507,9 @@
             f32((4 * band, lanes)), f32((4 * band, lanes)), f32((4 * band, lanes)),
             f32((edge_rows, lanes)), f32((edge_rows, lanes)),
             f32((3, edge_rows, lanes)), f32((3, edge_rows, lanes)),
-            f32((2 * fields, T * band, lanes)), f32((rank // 2, lanes)), f32((rank // 2, lanes)),
-            f32((n_lat - 1, rank // 2, lanes)), f32((n_lon - 1, rank // 2, lanes)),
+            f32((2 * fields, T * band, lanes)),
             dma((2, groups)), dma((2, groups)), dma((2,)), dma((2,)),
             dma((3,)), dma((3,)), dma((3,)), dma((3,)),
-            dma((n_lat - 1,)), dma((n_lat - 1,)), dma((n_lon - 1,)), dma((n_lon - 1,)),
         ],
         compiler_params=pltpu.CompilerParams(
             collective_id=0, has_side_effects=True, vmem_limit_bytes=32 * 1024 * 1024
@@ -508,6 +518,19 @@
         in_hbm(background.reshape(fields * band, lanes)), in_hbm(factor.reshape(rows, lanes)), in_hbm(depth),
         in_hbm(cells.reshape(1, slots)), count.reshape(1, 1), in_hbm(values.reshape(1, slots)), in_hbm(error.reshape(1, slots)),
     )
+    gram = pl.pallas_call(
+        functools.partial(total, n_lat, n_lon),
+        out_shape=jax.ShapeDtypeStruct(gram.shape, jnp.float32),
+        in_specs=[vmem],
+        out_specs=vmem,
+        scratch_shapes=[
+            f32(gram.shape), f32((n_lat - 1, *gram.shape)), f32((n_lon - 1, *gram.shape)),
+            dma((n_lat - 1,)), dma((n_lat - 1,)), dma((n_lon - 1,)), dma((n_lon - 1,)),
+        ],
+        compiler_params=pltpu.CompilerParams(
+            collective_id=1, has_side_effects=True, vmem_limit_bytes=4 * 1024 * 1024
+        ),
+    )(gram)
     updated, analysis = pl.pallas_call(
         functools.partial(transform, rank),
         out_shape=(

time: 26.1 us -> 28.7 us (1.100)
  Pallas kernels: 24.7 us -> 27.3 us
    pallas_call x0 -> x1, Pallas kernels: none -> 11.3 us  [per_device(): pl.pallas_call(functools.partial(total, n_lat, n_lon), out_shape=jax.Shap...]
    pallas_call x1, Pallas kernels: 22.7 us -> 14 us  [per_device(): pl.pallas_call(functools.partial(kernel, n_lat, n_lon, rank), out_shape=(...]
where the time goes in v5:
time: 28.7 us; the launch traced here: 28.6 us
  Pallas kernels  27.3 us (95%)
  between operations  1.29 us (4%)
    pallas_call x1, Pallas kernels, per_device(): pl.pallas_call(functools.partial(kernel, n_lat, n_lon, rank), out_shape=(...  14 us
    pallas_call x1, Pallas kernels, per_device(): pl.pallas_call(functools.partial(total, n_lat, n_lon), out_shape=jax.Shap...  11.3 us
    pallas_call x1, Pallas kernels, per_device(): pl.pallas_call(functools.partial(transform, rank), out_shape=(jax.ShapeDt...  1.96 us

profile of v5, /device:TPU:0, one launch (start us, length us, event | category | flops | bytes accessed | tf_op | source)
XLA Modules:
  0.0 28.6 jit_solution(9677389816165134408)
XLA Ops:
  1.3 14.0 %shard_map.86 = (f32[24,32,128]{2,1,0:T(8,128)S(1)}, f32[24,128]{1,0:T(8,128)S(1)}, f32[16,128]{1,0:T(8,128)S(1)}) custom-call(f32[24,128]{1,0:T(8,128)} %bitcast.10, f32[768,128]{1,0:T(8,128)} %bitcast.9, f32[8,128]{1,0:T(8,128)} %depth_hbm.1, s32[1,256]{1,0:T(1,128)} %bitcast.11, s32[1,1]{1,0:T(1,128)} %bitcast.8.count_hbm, f32[1,256]{1,0:T(1,128)} %bitcast.12, ...), custom_call_target="tpu_custom_call" | custom-call | tf_op jit(solution)/shard_map/pallas_call | solution.py:494
  15.3 11.3 %shard_map.87.gram_ref = f32[16,128]{1,0:T(8,128)S(1)} custom-call(f32[16,128]{1,0:T(8,128)S(1)} %get-tuple-element.9.part_ref), custom_call_target="tpu_custom_call" | custom-call | tf_op jit(solution)/shard_map/pallas_call | solution.py:521
  26.6 2.0 %shard_map.88 = (f32[24,128]{1,0:T(8,128)}, f32[768,128]{1,0:T(8,128)}) custom-call(f32[24,32,128]{2,1,0:T(8,128)S(1)} %get-tuple-element.7.fc, f32[24,128]{1,0:T(8,128)S(1)} %get-tuple-element.8.mean_ref, f32[16,128]{1,0:T(8,128)S(1)} %shard_map.87.gram_ref), custom_call_target="tpu_custom_call" | custom-call | tf_op jit(solution)/shard_map/pallas_call | solution.py:534

commit v6 on v3

--- a/solution.py
+++ b/solution.py
@@ -50,6 +50,10 @@
     return h, e, n
 
 
+def pair_of(n_lon):
+    return 2 if n_lon % 2 == 0 else 1
+
+
 def kernel(
     n_lat, n_lon, rank,
     mean_hbm, fac_hbm, depth_hbm, cells_hbm, count_hbm, vals_hbm, err_hbm,
@@ -73,11 +77,27 @@
     def at(dlat, dlon):
         return (lax.rem(lat + dlat + n_lat, n_lat), lax.rem(lon + dlon + n_lon, n_lon))
 
-    diagonals = [(a, b) for a in (-1, 1) for b in (-1, 1)]
-    peers = [(a, 0) for a in range(1, n_lat)] + [(0, b) for b in range(1, n_lon)] + diagonals
+    inner = pair_of(n_lon)
+    outer, plane = n_lon // inner, n_lat * inner
+    lon_in, lon_out = lax.rem(lon, inner), lon // inner
+    place = lat * inner + lon_in
+
+    def in_plane(o):
+        peer = lax.rem(place + o, plane)
+        return (peer // inner, lon_out * inner + lax.rem(peer, inner))
+
+    def in_line(o):
+        return (lat, lax.rem(lon_out + o, outer) * inner + lon_in)
+
+    if inner == 2:
+        beyond = 2 * lon_in - 1
+        rest = [at(a, beyond) for a in (0, -1, 1)]
+    else:
+        rest = [at(a, b) for a in (-1, 1) for b in (-1, 1)]
+    peers = [in_plane(o) for o in range(1, plane)] + rest + [in_line(o) for o in range(1, outer)]
     barrier = pltpu.get_barrier_semaphore()
-    for a, b in peers:
-        pl.semaphore_signal(barrier, inc=1, device_id=at(a, b), device_id_type=MESH)
+    for peer in peers:
+        pl.semaphore_signal(barrier, inc=1, device_id=peer, device_id_type=MESH)
 
     has_up, has_dn = lat > 0, lat < n_lat - 1
     fetched = [
@@ -364,23 +384,23 @@
 
     p1[...] = mine
     def lat_copy(o):
-        return remote(p1, ar1.at[o - 1], s1.at[o - 1], r1.at[o - 1], at(o, 0))
+        return remote(p1, ar1.at[o - 1], s1.at[o - 1], r1.at[o - 1], in_plane(o))
     def lon_copy(o):
-        return remote(p2, ar2.at[o - 1], s2.at[o - 1], r2.at[o - 1], at(0, o))
-    for o in range(1, n_lat):
+        return remote(p2, ar2.at[o - 1], s2.at[o - 1], r2.at[o - 1], in_line(o))
+    for o in range(1, plane):
         lat_copy(o).start()
     merge(1)
     merge(2)
     for f in range(3):
         for r in range(band):
             mean_out[f * band + r : f * band + r + 1, :] = mean[f][T * r : T * r + 1]
-    for o in range(1, n_lat):
+    for o in range(1, plane):
         lat_copy(o).wait_recv()
         mine = mine + ar1[o - 1]
     p2[...] = mine
-    for o in range(1, n_lon):
+    for o in range(1, outer):
         lon_copy(o).start()
-    for o in range(1, n_lon):
+    for o in range(1, outer):
         lon_copy(o).wait_recv()
         mine = mine + ar2[o - 1]
 
@@ -396,9 +416,9 @@
             edge_copy(False, 2 * side).wait_send()
     edge_copy(True, 1).wait_send()
     edge_copy(False, 1).wait_send()
-    for o in range(1, n_lat):
+    for o in range(1, plane):
         lat_copy(o).wait_send()
-    for o in range(1, n_lon):
+    for o in range(1, outer):
         lon_copy(o).wait_send()
 
 
@@ -474,6 +494,7 @@
     rows = rank * fields * band
     slots = cells.shape[0]
     assert band == T and 2 * STEPS <= band and rank % T == 0 and fields == 3
+    plane, outer = n_lat * pair_of(n_lon), n_lon // pair_of(n_lon)
     edge_rows = T * (fields * band * groups * 2 * STEPS // lanes + 1)
     vmem = pl.BlockSpec(memory_space=pltpu.VMEM)
     f32 = functools.partial(pltpu.VMEM, dtype=jnp.float32)
@@ -496,10 +517,10 @@
             f32((edge_rows, lanes)), f32((edge_rows, lanes)),
             f32((3, edge_rows, lanes)), f32((3, edge_rows, lanes)),
             f32((2 * fields, T * band, lanes)), f32((rank // 2, lanes)), f32((rank // 2, lanes)),
-            f32((n_lat - 1, rank // 2, lanes)), f32((n_lon - 1, rank // 2, lanes)),
+            f32((plane - 1, rank // 2, lanes)), f32((outer - 1, rank // 2, lanes)),
             dma((2, groups)), dma((2, groups)), dma((2,)), dma((2,)),
             dma((3,)), dma((3,)), dma((3,)), dma((3,)),
-            dma((n_lat - 1,)), dma((n_lat - 1,)), dma((n_lon - 1,)), dma((n_lon - 1,)),
+            dma((plane - 1,)), dma((plane - 1,)), dma((outer - 1,)), dma((outer - 1,)),
         ],
         compiler_params=pltpu.CompilerParams(
             collective_id=0, has_side_effects=True, vmem_limit_bytes=32 * 1024 * 1024

time: 26.1 us -> 26.2 us (level)
  no operation moved by 1% of the time
where the time goes in v6:
time: 26.2 us; the launch traced here: 26 us
  Pallas kernels  24.7 us (94%)
  between operations  1.29 us (5%)
    pallas_call x1, Pallas kernels, per_device(): pl.pallas_call(functools.partial(kernel, n_lat, n_lon, rank), out_shape=(...  22.8 us
    pallas_call x1, Pallas kernels, per_device(): pl.pallas_call(functools.partial(transform, rank), out_shape=(jax.ShapeDt...  1.96 us

profile of v6, /device:TPU:0, one launch (start us, length us, event | category | flops | bytes accessed | tf_op | source)
XLA Modules:
  0.0 26.0 jit_solution(7027105782834895743)
XLA Ops:
  1.3 22.8 %shard_map.86 = (f32[24,32,128]{2,1,0:T(8,128)S(1)}, f32[24,128]{1,0:T(8,128)S(1)}, f32[16,128]{1,0:T(8,128)S(1)}) custom-call(f32[24,128]{1,0:T(8,128)} %bitcast.10, f32[768,128]{1,0:T(8,128)} %bitcast.9, f32[8,128]{1,0:T(8,128)} %depth_hbm.1, s32[1,256]{1,0:T(1,128)} %bitcast.11, s32[1,1]{1,0:T(1,128)} %bitcast.8.count_hbm, f32[1,256]{1,0:T(1,128)} %bitcast.12, ...), custom_call_target="tpu_custom_call" | custom-call | tf_op jit(solution)/shard_map/pallas_call | solution.py:503
  24.1 2.0 %shard_map.87 = (f32[24,128]{1,0:T(8,128)}, f32[768,128]{1,0:T(8,128)}) custom-call(f32[24,32,128]{2,1,0:T(8,128)S(1)} %get-tuple-element.7.fc, f32[24,128]{1,0:T(8,128)S(1)} %get-tuple-element.8.mean_ref, f32[16,128]{1,0:T(8,128)S(1)} %get-tuple-element.9.gram_ref), custom_call_target="tpu_custom_call" | custom-call | tf_op jit(solution)/shard_map/pallas_call | solution.py:532

commit v7 on v2

--- a/solution.py
+++ b/solution.py
@@ -74,7 +74,7 @@
         return (lax.rem(lat + dlat + n_lat, n_lat), lax.rem(lon + dlon + n_lon, n_lon))
 
     diagonals = [(a, b) for a in (-1, 1) for b in (-1, 1)]
-    peers = [(a, 0) for a in range(1, n_lat)] + [(0, b) for b in range(1, n_lon)] + diagonals
+    peers = [(0, b) for b in range(n_lon - 1, 0, -1)] + diagonals + [(a, 0) for a in range(1, n_lat)]
     barrier = pltpu.get_barrier_semaphore()
     for a, b in peers:
         pl.semaphore_signal(barrier, inc=1, device_id=at(a, b), device_id_type=MESH)

time: 26 us -> 26 us (level)
  no operation moved by 1% of the time
where the time goes in v7:
time: 26 us; the launch traced here: 25.9 us
  Pallas kernels  24.6 us (95%)
  between operations  1.29 us (5%)
    pallas_call x1, Pallas kernels, per_device(): pl.pallas_call(functools.partial(kernel, n_lat, n_lon, rank), out_shape=(...  22.6 us
    pallas_call x1, Pallas kernels, per_device(): pl.pallas_call(functools.partial(transform, rank), out_shape=(jax.ShapeDt...  1.96 us

profile of v7, /device:TPU:0, one launch (start us, length us, event | category | flops | bytes accessed | tf_op | source)
XLA Modules:
  0.0 25.9 jit_solution(16262118124206648374)
XLA Ops:
  1.3 22.6 %shard_map.86 = (f32[24,32,128]{2,1,0:T(8,128)S(1)}, f32[24,128]{1,0:T(8,128)S(1)}, f32[16,128]{1,0:T(8,128)S(1)}) custom-call(f32[24,128]{1,0:T(8,128)} %bitcast.10, f32[768,128]{1,0:T(8,128)} %bitcast.9, f32[8,128]{1,0:T(8,128)} %depth_hbm.1, s32[1,256]{1,0:T(1,128)} %bitcast.11, s32[1,1]{1,0:T(1,128)} %bitcast.8.count_hbm, f32[1,256]{1,0:T(1,128)} %bitcast.12, ...), custom_call_target="tpu_custom_call" | custom-call | tf_op jit(solution)/shard_map/pallas_call | solution.py:453
  23.9 2.0 %shard_map.87 = (f32[24,128]{1,0:T(8,128)}, f32[768,128]{1,0:T(8,128)}) custom-call(f32[24,32,128]{2,1,0:T(8,128)S(1)} %get-tuple-element.7.fc, f32[24,128]{1,0:T(8,128)S(1)} %get-tuple-element.8.mean_ref, f32[16,128]{1,0:T(8,128)S(1)} %get-tuple-element.9.gram_ref), custom_call_target="tpu_custom_call" | custom-call | tf_op jit(solution)/shard_map/pallas_call | solution.py:482
